TPU v7x, 256 devices: a whole 4x4x8 slice. The times are simulated.
256 devices in a mesh: depth: 8 (over z_hi, core), tile: 32 (over z_lo, y, x).
Axes of the slice: x: 4, y: 4, z: 8 (z_hi: 4, z_lo: 2; z = z_hi * 2 + z_lo), core: 2. Of those that a mesh axis runs over, the one named last changes fastest.
Arguments:
- first_factor_embedding: bfloat16 [1024, 64, 32], P('depth', 'tile'), may hold values from -6 to 6
- second_factor_embedding: bfloat16 [1024, 3072, 32], P('depth', 'tile'), may hold values from -6 to 6
- final_linear_matrix: bfloat16 [1024, 128], replicated, may hold values from -4.1875 to 4.1875
- output_bias: float32 [128], replicated, may hold values from -3 to 3
Outputs:
- pair_update: bfloat16 [64, 3072, 128], P('depth', 'tile')
All inputs are finite; a program needn't handle non-finite values.
Results may differ from a plain program's by a relative error of at most 0.01.
Values may be sent and summed in bfloat16 or wider, within the bound.
No kernel may reach another device: no remote copies, remote signals or barrier semaphores. Data moves between devices by JAX's collectives and lax.ppermute only.
A program may use at most 192 MiB of HBM per device.

v0:
```python
import jax
import jax.numpy as jnp
from jax import lax
from jax.sharding import PartitionSpec as P


def project_split(values, weight):
    upper = values.astype(jnp.bfloat16)
    lower = (values - upper.astype(jnp.float32)).astype(jnp.bfloat16)
    first = jnp.einsum("ijk,kd->ijd", upper, weight, preferred_element_type=jnp.float32)
    second = jnp.einsum("ijk,kd->ijd", lower, weight, preferred_element_type=jnp.float32)
    return first + second


def local(first_factor_embedding, second_factor_embedding, final_linear_matrix, output_bias):
    slab_block = lax.all_gather(first_factor_embedding, "tile", axis=1, tiled=True)
    alignment_rows = first_factor_embedding.shape[0] * lax.axis_size("depth")
    rows_here = slab_block.shape[1] // lax.axis_size("depth")
    pair_width = second_factor_embedding.shape[1]
    outer_product = jnp.einsum(
        "oaw,odf->adwf", slab_block, second_factor_embedding, preferred_element_type=jnp.float32
    )
    summed = lax.psum_scatter(
        outer_product.reshape(lax.axis_size("depth") * rows_here, pair_width, -1),
        "depth",
        scatter_dimension=0,
        tiled=True,
    )
    mixed = project_split(summed / alignment_rows, final_linear_matrix)
    return (mixed + output_bias).astype(jnp.bfloat16)


def solution(mesh):
    in_specs = (P("depth", "tile", None), P("depth", "tile", None), P(), P())
    out_specs = P("depth", "tile", None)
    return jax.shard_map(local, mesh=mesh, in_specs=in_specs, out_specs=out_specs, check_vma=False)
```

profile of v0, /device:TPU:38, one launch (start us, length us, event | category | flops | bytes accessed | tf_op | source)
XLA Modules:
  0.0 420.4 jit_solution(7433021644717379080)
XLA Ops:
  6.5 0.0 copy-start
  6.5 0.0 reduce-scatter.2.cloned.1.call-start
  6.5 74.0 %all_gather.3 = bf16[128,64,32]{0,2,1:T(8,128)(2,1)S(1)} all-gather(bf16[128,2,32]{0,2,1:T(8,128)(2,1)} %param.4), channel_id=1, replica_groups=mesh['depth'=8,'tile'=32] {'tile'}, dimensions={1}, use_global_device_ids=true | all-gather | bytes 540672 | tf_op jit(solution)/shard_map/all_gather | solution.py:16
  80.6 0.0 copy-done
  80.6 19.4 %fusion.7 = f32[96,32,64,32]{2,1,3,0:T(8,128)} fusion(bf16[128,96,32]{0,2,1:T(8,128)(2,1)S(1)} %copy-done, bf16[128,64,32]{0,2,1:T(8,128)(2,1)S(1)} %all_gather.3), kind=kOutput, calls=%fused_computation.9 | convolution fusion | flops 1610612736 | bytes 26476544 | tf_op jit(solution)/shard_map/oaw,odf->adwf/dot_general | solution.py:20
  99.9 38.8 %copy.8 = f32[64,96,1024]{2,1,0:T(8,128)} copy(f32[64,96,1024]{0,2,1:T(8,128)} %bitcast.16) | data formatting | bytes 50331648 | tf_op jit(solution)/shard_map/reshape | solution.py:24
  138.8 0.0 copy-start.3
  138.8 0.0 reduce-scatter.2.cloned.1.call-update
  138.8 0.0 copy-start.4
  138.8 0.0 copy-start.1
  138.8 270.6 %reduce-scatter.2.cloned.1.call-done = f32[8,96,1024]{2,1,0:T(8,128)} async-done(((f32[64,96,1024]{2,1,0:T(8,128)}), f32[8,96,1024]{2,1,0:T(8,128)}) %reduce-scatter.2.cloned.1.call-update) | async-done | bytes 3145744 | tf_op jit(solution)/shard_map/reduce_scatter | solution.py:23
  409.5 0.0 copy-done.3
  409.5 0.0 copy-start.2
  409.5 2.6 fusion
  412.1 0.0 copy-done.4
  412.1 0.2 copy-done.2
  412.3 1.3 fusion.6
  413.6 0.0 copy-done.1
Async XLA Ops:
  6.5 74.0 %copy-start = (bf16[128,96,32]{0,2,1:T(8,128)(2,1)S(1)}, bf16[128,96,32]{0,2,1:T(8,128)(2,1)}, u32[]{:S(2)}) copy-start(bf16[128,96,32]{0,2,1:T(8,128)(2,1)} %param.5) | copy-start | bytes 2359300
  6.5 402.9 %reduce-scatter.2.cloned.1.call-start = ((), (), s32[]{:S(2)}) async-start(), calls=%async_computation.1 | async-start | bytes 28311552 | tf_op jit(solution)/shard_map/reduce_scatter | solution.py:23
  138.8 270.7 %copy-start.3 = (bf16[1024,128]{1,0:T(8,128)(2,1)S(1)}, bf16[1024,128]{1,0:T(8,128)(2,1)}, u32[]{:S(2)}) copy-start(bf16[1024,128]{1,0:T(8,128)(2,1)} %param.6) | copy-start | bytes 786436
  138.8 273.3 %copy-start.4 = (f32[128]{0:T(128)S(1)}, f32[128]{0:T(128)}, u32[]{:S(2)}) copy-start(f32[128]{0:T(128)} %param.7) | copy-start | bytes 1540
  138.8 274.7 %copy-start.1 = (bf16[128,96,32]{0,2,1:T(8,128)(2,1)S(1)}, bf16[128,96,32]{0,2,1:T(8,128)(2,1)}, u32[]{:S(2)}) copy-start(bf16[128,96,32]{0,2,1:T(8,128)(2,1)} %param.5) | copy-start | bytes 2359300
  409.5 2.8 copy-start.2
Sparse Core Ops, SparseCore 0:
  138.9 270.4 reduce-scatter.1
where the time goes:
time: 421 us; the launch traced here: 420 us
  waiting for transfers between devices  271 us (64%)
  blocking collectives  74 us (18%)
  local copies, waits for them, and re-layouts  39.1 us (9%)
  matrix products  23.2 us (6%)
  between operations  13.4 us (3%)
    reduce_scatter x1, waiting for transfers between devices, local(): lax.psum_scatter(outer_product.reshape(lax.axis_size('depth') * rows_here...  271 us
    all_gather x1, blocking collectives, local(): lax.all_gather(first_factor_embedding, 'tile', axis=1, tiled=True)  74 us
    reshape x1, local copies, waits for them, and re-layouts, local(): outer_product.reshape(lax.axis_size('depth') * rows_here, pair_width, -1)  38.8 us
    dot_general x1, matrix products, local(): jnp.einsum('oaw,odf->adwf', slab_block, second_factor_embedding, preferre...  19.4 us
  transfers between devices with their start and end apart: 1, of which 1 were waited for; matrix products, arithmetic and copies ran while one was open for 0% of the time, Pallas kernels for 0%

commit v1 on v0

v1 whole, which is shorter than its diff:
```python
import functools

import jax
import jax.numpy as jnp
from jax import lax
from jax.experimental import pallas as pl
from jax.experimental.pallas import tpu as pltpu
from jax.sharding import Mesh, PartitionSpec as P

FEATS = 32
ROWS = 8
LANES = 128
RING = 4
DEPTH_AXES = ("zh", "core")
TILE_AXES = ("zl", "y", "x")


def prep_kernel(own_ref, other_ref, out_ref, wide_ref):
    cols = own_ref.shape[0] // FEATS
    for half, ref in ((0, own_ref), (1, other_ref)):
        wide_ref[...] = ref[...].astype(jnp.float32)
        for f in range(FEATS):
            picked = wide_ref[pl.ds(f, cols, stride=FEATS), :]
            out_ref[f, 0:cols, half * LANES:(half + 1) * LANES] = picked.astype(jnp.bfloat16)
    out_ref[:, cols:, :] = jnp.zeros((FEATS, LANES - cols, 2 * LANES), jnp.bfloat16)


def prep(own, other):
    cols = own.shape[0]
    whole = pl.BlockSpec(memory_space=pltpu.VMEM)
    return pl.pallas_call(
        prep_kernel,
        out_shape=jax.ShapeDtypeStruct((FEATS, LANES, 2 * LANES), jnp.bfloat16),
        scratch_shapes=[pltpu.VMEM((cols * FEATS, LANES), jnp.float32)],
        in_specs=[whole, whole],
        out_specs=whole,
        compiler_params=pltpu.CompilerParams(vmem_limit_bytes=32 << 20),
        cost_estimate=pl.CostEstimate(flops=0, bytes_accessed=8 << 20, transcendentals=0),
        name="prep",
    )(own.reshape(cols * FEATS, LANES), other.reshape(cols * FEATS, LANES))


def pair_kernel(chunks, idx_ref, own_ref, other_ref, b_ref, w_ref, out_ref):
    width = ROWS * FEATS
    a = jnp.concatenate(
        [own_ref[...].reshape(width, LANES), other_ref[...].reshape(width, LANES)], axis=1
    )
    feats = FEATS // chunks
    total = None
    for c in range(chunks):
        b = b_ref[c * feats:(c + 1) * feats].reshape(feats * LANES, 2 * LANES)
        outer = lax.dot_general(
            a, b, (((1,), (1,)), ((), ())), preferred_element_type=jnp.float32
        ).astype(jnp.bfloat16)
        stacked = jnp.concatenate(
            [
                jnp.concatenate(
                    [
                        outer[r * FEATS:(r + 1) * FEATS, f * LANES:(f + 1) * LANES]
                        for r in range(ROWS)
                    ],
                    axis=1,
                )
                for f in range(feats)
            ],
            axis=0,
        )
        lanes = feats * FEATS
        part = jnp.dot(
            w_ref[:, c * lanes:(c + 1) * lanes], stacked, preferred_element_type=jnp.float32
        )
        total = part if total is None else total + part
    cols = out_ref.shape[1]
    for r in range(ROWS):
        out_ref[r] = total[:, r * LANES:(r + 1) * LANES].T[:cols].astype(jnp.bfloat16)


def pair_block(idx, own, other, b, wt, cols):
    rows = pl.BlockSpec(
        (None, None, ROWS, FEATS, LANES), lambda i, idx: (idx[0], idx[1], 0, 0, 0)
    )
    return pl.pallas_call(
        functools.partial(pair_kernel, 4),
        grid_spec=pltpu.PrefetchScalarGridSpec(
            num_scalar_prefetch=1,
            grid=(1,),
            in_specs=[
                rows,
                rows,
                pl.BlockSpec(b.shape, lambda i, idx: (0, 0, 0)),
                pl.BlockSpec(wt.shape, lambda i, idx: (0, 0)),
            ],
            out_specs=pl.BlockSpec((ROWS, cols, LANES), lambda i, idx: (0, 0, 0)),
        ),
        out_shape=jax.ShapeDtypeStruct((ROWS, cols, LANES), jnp.bfloat16),
        compiler_params=pltpu.CompilerParams(vmem_limit_bytes=40 << 20),
        cost_estimate=pl.CostEstimate(flops=3 << 30, bytes_accessed=4 << 20, transcendentals=0),
        name="pair_block",
    )(idx, own, other, b, wt)


def local(first, second, matrix, bias):
    tiles = 32
    sequences = 1024
    swap = [(0, 1), (1, 0)]
    zh = lax.axis_index("zh")
    core = lax.axis_index("core")
    at = jnp.transpose(first, (1, 2, 0))
    bt = jnp.transpose(second, (1, 2, 0))
    cols = bt.shape[0]
    b_other = lax.ppermute(bt, "core", swap)
    spread = jnp.broadcast_to(at[None], (tiles,) + at.shape)
    a_own = lax.all_to_all(spread, TILE_AXES, split_axis=0, concat_axis=0, tiled=True)
    a_own = a_own.reshape(RING, 2, ROWS, FEATS, LANES)
    a_other = lax.ppermute(a_own, "core", swap)
    b = prep(bt, b_other)
    wt = matrix.reshape(FEATS, FEATS, LANES).transpose(2, 1, 0).reshape(LANES, FEATS * FEATS)

    def block(k):
        idx = jnp.stack([(zh + k) % RING, core]).astype(jnp.int32)
        return pair_block(idx, a_own, a_other, b, wt, cols)

    total = None
    received = []
    for k in (2, 1, 3):
        part = block(k)
        received.append(lax.ppermute(part, "zh", [(i, (i + k) % RING) for i in range(RING)]))
    total = block(0).astype(jnp.float32)
    for part in received:
        total = total + part.astype(jnp.float32)
    return (total * (1.0 / sequences) + bias).astype(jnp.bfloat16)


def solution(mesh):
    fine = Mesh(
        mesh.devices.reshape(RING, 2, 2, 4, 4), DEPTH_AXES + TILE_AXES
    )
    in_specs = (P(DEPTH_AXES, TILE_AXES, None), P(DEPTH_AXES, TILE_AXES, None), P(), P())
    out_specs = P(DEPTH_AXES, TILE_AXES, None)
    return jax.shard_map(local, mesh=fine, in_specs=in_specs, out_specs=out_specs, check_vma=False)
```

time: 421 us -> 55.1 us (0.13)
  the two profiles are of different devices: /device:TPU:38 before, /device:TPU:1 now
where the time goes in v1:
time: 55.1 us; the launch traced here: 54.8 us
  starting transfers between devices  22.7 us (41%)
  waiting for transfers between devices  17.5 us (32%)
  Pallas kernels  10.5 us (19%)
  local copies, waits for them, and re-layouts  2.92 us (5%)
  other arithmetic  1.11 us (2%)
    ppermute x3, starting transfers between devices, local(): lax.ppermute(part, 'zh', [(i, (i + k) % RING) for i in range(RING)])  9.84 us
    all_to_all x1, starting transfers between devices, local(): lax.all_to_all(spread, TILE_AXES, split_axis=0, concat_axis=0, tiled=True)  9.22 us
    all_to_all x1, waiting for transfers between devices, local(): lax.all_to_all(spread, TILE_AXES, split_axis=0, concat_axis=0, tiled=True)  8.88 us
    ppermute x3, waiting for transfers between devices, local(): lax.ppermute(part, 'zh', [(i, (i + k) % RING) for i in range(RING)])  8.58 us
    pallas_call x4, Pallas kernels, pair_block(): pl.pallas_call(functools.partial(pair_kernel, 4), grid_spec=pltpu.Prefetc...  8.12 us
    ppermute x1, starting transfers between devices, local(): a_other = lax.ppermute(a_own, 'core', swap)  2.6 us
    pallas_call x1, Pallas kernels, prep(): pl.pallas_call(prep_kernel, out_shape=jax.ShapeDtypeStruct((FEATS, LANES,...  2.41 us
    broadcast_in_dim x1, local copies, waits for them, and re-layouts, local(): spread = jnp.broadcast_to(at[None], (tiles,) + at.shape)  1.71 us
  transfers between devices with their start and end apart: 6, of which 3 were waited for; matrix products, arithmetic and copies ran while one was open for 3% of the time, Pallas kernels for 16%

profile of v1, /device:TPU:1, one launch (start us, length us, event | category | flops | bytes accessed | tf_op | source)
XLA Modules:
  0.0 54.8 jit_solution(13907538043328127731)
XLA Ops:
  0.0 0.0 copy-start
  0.0 1.7 %broadcast_in_dim.2 = bf16[32,2,32,128]{3,2,1,0:T(8,128)(2,1)} broadcast(bf16[2,32,128]{2,1,0:T(8,128)(2,1)} %bitcast.25), dimensions={1,2,3} | broadcast | bytes 540672 | tf_op jit(solution)/shard_map/broadcast_in_dim | solution.py:112
  1.7 9.2 %all-to-all-start = ((bf16[32,2,32,128]{3,2,1,0:T(8,128)(2,1)}), bf16[32,2,32,128]{3,2,1,0:T(8,128)(2,1)S(1)}, u32[]{:S(2)}, u32[]{:S(2)}) async-start(bf16[32,2,32,128]{3,2,1,0:T(8,128)(2,1)} %broadcast_in_dim.2), calls=%async_computation | async-start | bytes 1048576 | tf_op jit(solution)/shard_map/all_to_all | solution.py:113
  10.9 1.0 %collective-permute-start.1 = (bf16[96,32,128]{2,1,0:T(8,128)(2,1)}, bf16[96,32,128]{2,1,0:T(8,128)(2,1)S(1)}, u32[]{:S(2)}, u32[]{:S(2)}) collective-permute-start(bf16[96,32,128]{2,1,0:T(8,128)(2,1)} %bitcast.15), channel_id=1, source_target_pairs={{0,32},{32,0},{1,33},{33,1},{2,34},{34,2},{3,35},{35,3},{4,36},{36... | collective-permute-start | bytes 2359304 | tf_op jit(solution)/shard_map/ppermute | solution.py:111
  12.0 8.9 %all-to-all-done = bf16[32,2,32,128]{3,2,1,0:T(8,128)(2,1)S(1)} async-done(((bf16[32,2,32,128]{3,2,1,0:T(8,128)(2,1)}), bf16[32,2,32,128]{3,2,1,0:T(8,128)(2,1)S(1)}, u32[]{:S(2)}, u32[]{:S(2)}) %all-to-all-start) | async-done | bytes 524320 | tf_op jit(solution)/shard_map/all_to_all | solution.py:113
  20.9 2.6 %collective-permute-start = (bf16[4,2,8,32,128]{4,3,2,1,0:T(8,128)(2,1)S(1)}, bf16[4,2,8,32,128]{4,3,2,1,0:T(8,128)(2,1)S(1)}, u32[]{:S(2)}, u32[]{:S(2)}) collective-permute-start(bf16[4,2,8,32,128]{4,3,2,1,0:T(8,128)(2,1)S(1)} %bitcast.18), channel_id=1, source_target_pairs={{0,32},{32,0},{1,33},{33,1},{2,34},{34,2},{3,35},{35,3},{4,36},{36... | collective-permute-start | bytes 1572872 | tf_op jit(solution)/shard_map/ppermute | solution.py:115
  23.5 1.1 %copy.10 = bf16[128,32,32]{0,2,1:T(8,128)(2,1)S(1)} copy(bf16[128,32,32]{0,1,2:T(8,128)(2,1)} %bitcast.24) | data formatting | bytes 524288 | tf_op jit(solution)/shard_map/transpose | solution.py:117
  24.5 0.1 copy.11.w_ref
  24.7 0.1 pad_add_fusion.1.idx_ref
  24.8 0.1 pad_add_fusion.2.idx_ref
  24.9 0.1 pad_add_fusion.idx_ref
  24.9 0.1 pad_add_fusion.3.idx_ref
  25.0 0.0 collective-permute-done.1
  25.0 0.0 copy-done
  25.0 2.4 %prep.1.b_ref = bf16[32,128,256]{2,1,0:T(8,128)(2,1)S(1)} custom-call(bf16[3072,128]{1,0:T(8,128)(2,1)S(1)} %bitcast.16, bf16[3072,128]{1,0:T(8,128)(2,1)S(1)} %bitcast.17), custom_call_target="tpu_custom_call" | custom-call | bytes 8388608 | tf_op jit(solution)/shard_map/prep/pallas_call | solution.py:31
  27.4 0.0 collective-permute-done.other_ref
  27.4 2.0 %pair_block.5 = bf16[8,96,128]{2,1,0:T(8,128)(2,1)S(1)} custom-call(s32[2]{0:T(128)S(1)} %pad_add_fusion.1.idx_ref, bf16[4,2,8,32,128]{4,3,2,1,0:T(8,128)(2,1)S(1)} %bitcast.19, bf16[4,2,8,32,128]{4,3,2,1,0:T(8,128)(2,1)S(1)} %collective-permute-done.other_ref, bf16[32,128,256]{2,1,0:T(8,128)(2,1)S(1)} %prep.1.b_ref, bf16[128,1024]{1,0:T(8,128)(2,1)S(1)} %copy.11.w_ref), custom_call_target="tpu_custom_call" | custom-call | flops 3221225472 | bytes 4194304 | tf_op jit(solution)/shard_map/pair_block/pallas_call | solution.py:82
  29.5 6.1 %collective-permute-start.2 = (bf16[8,96,128]{2,1,0:T(8,128)(2,1)S(1)}, bf16[8,96,128]{2,1,0:T(8,128)(2,1)S(1)}, u32[]{:S(2)}, u32[]{:S(2)}) collective-permute-start(bf16[8,96,128]{2,1,0:T(8,128)(2,1)S(1)} %pair_block.5), channel_id=1, source_target_pairs={{0,128},{64,192},{128,0},{192,64},{1,129},{65,193},{129,1},{193,65... | collective-permute-start | bytes 589832 | tf_op jit(solution)/shard_map/ppermute | solution.py:127
  35.6 2.0 %pair_block.6 = bf16[8,96,128]{2,1,0:T(8,128)(2,1)S(1)} custom-call(s32[2]{0:T(128)S(1)} %pad_add_fusion.2.idx_ref, bf16[4,2,8,32,128]{4,3,2,1,0:T(8,128)(2,1)S(1)} %bitcast.20, bf16[4,2,8,32,128]{4,3,2,1,0:T(8,128)(2,1)S(1)} %collective-permute-done.other_ref, bf16[32,128,256]{2,1,0:T(8,128)(2,1)S(1)} %prep.1.b_ref, bf16[128,1024]{1,0:T(8,128)(2,1)S(1)} %copy.11.w_ref), custom_call_target="tpu_custom_call" | custom-call | flops 3221225472 | bytes 4194304 | tf_op jit(solution)/shard_map/pair_block/pallas_call | solution.py:82
  37.6 1.3 %collective-permute-start.3 = (bf16[8,96,128]{2,1,0:T(8,128)(2,1)S(1)}, bf16[8,96,128]{2,1,0:T(8,128)(2,1)S(1)}, u32[]{:S(2)}, u32[]{:S(2)}) collective-permute-start(bf16[8,96,128]{2,1,0:T(8,128)(2,1)S(1)} %pair_block.6), channel_id=1, source_target_pairs={{0,64},{64,128},{128,192},{192,0},{1,65},{65,129},{129,193},{193,1... | collective-permute-start | bytes 589832 | tf_op jit(solution)/shard_map/ppermute | solution.py:127
  38.9 2.0 %pair_block.7 = bf16[8,96,128]{2,1,0:T(8,128)(2,1)S(1)} custom-call(s32[2]{0:T(128)S(1)} %pad_add_fusion.3.idx_ref, bf16[4,2,8,32,128]{4,3,2,1,0:T(8,128)(2,1)S(1)} %bitcast.21, bf16[4,2,8,32,128]{4,3,2,1,0:T(8,128)(2,1)S(1)} %collective-permute-done.other_ref, bf16[32,128,256]{2,1,0:T(8,128)(2,1)S(1)} %prep.1.b_ref, bf16[128,1024]{1,0:T(8,128)(2,1)S(1)} %copy.11.w_ref), custom_call_target="tpu_custom_call" | custom-call | flops 3221225472 | bytes 4194304 | tf_op jit(solution)/shard_map/pair_block/pallas_call | solution.py:82
  40.9 0.0 copy-start.1
  40.9 2.5 %collective-permute-start.4 = (bf16[8,96,128]{2,1,0:T(8,128)(2,1)S(1)}, bf16[8,96,128]{2,1,0:T(8,128)(2,1)S(1)}, u32[]{:S(2)}, u32[]{:S(2)}) collective-permute-start(bf16[8,96,128]{2,1,0:T(8,128)(2,1)S(1)} %pair_block.7), channel_id=1, source_target_pairs={{0,192},{64,0},{128,64},{192,128},{1,193},{65,1},{129,65},{193,129... | collective-permute-start | bytes 589832 | tf_op jit(solution)/shard_map/ppermute | solution.py:127
  43.4 2.0 %pair_block.4 = bf16[8,96,128]{2,1,0:T(8,128)(2,1)S(1)} custom-call(s32[2]{0:T(128)S(1)} %pad_add_fusion.idx_ref, bf16[4,2,8,32,128]{4,3,2,1,0:T(8,128)(2,1)S(1)} %bitcast.22, bf16[4,2,8,32,128]{4,3,2,1,0:T(8,128)(2,1)S(1)} %collective-permute-done.other_ref, bf16[32,128,256]{2,1,0:T(8,128)(2,1)S(1)} %prep.1.b_ref, bf16[128,1024]{1,0:T(8,128)(2,1)S(1)} %copy.11.w_ref), custom_call_target="tpu_custom_call" | custom-call | flops 3221225472 | bytes 4194304 | tf_op jit(solution)/shard_map/pair_block/pallas_call | solution.py:82
  45.4 0.0 collective-permute-done.2
  45.5 4.3 %collective-permute-done.3 = bf16[8,96,128]{2,1,0:T(8,128)(2,1)S(1)} collective-permute-done((bf16[8,96,128]{2,1,0:T(8,128)(2,1)S(1)}, bf16[8,96,128]{2,1,0:T(8,128)(2,1)S(1)}, u32[]{:S(2)}, u32[]{:S(2)}) %collective-permute-start.3) | collective-permute-done | bytes 196640 | tf_op jit(solution)/shard_map/ppermute | solution.py:127
  49.8 4.2 %collective-permute-done.4 = bf16[8,96,128]{2,1,0:T(8,128)(2,1)S(1)} collective-permute-done((bf16[8,96,128]{2,1,0:T(8,128)(2,1)S(1)}, bf16[8,96,128]{2,1,0:T(8,128)(2,1)S(1)}, u32[]{:S(2)}, u32[]{:S(2)}) %collective-permute-start.4) | collective-permute-done | bytes 196640 | tf_op jit(solution)/shard_map/ppermute | solution.py:127
  54.0 0.0 copy-done.1
  54.0 0.8 %add_convert_fusion = bf16[8,96,128]{2,1,0:T(8,128)(2,1)} fusion(bf16[8,96,128]{2,1,0:T(8,128)(2,1)S(1)} %collective-permute-done.4, bf16[8,96,128]{2,1,0:T(8,128)(2,1)S(1)} %collective-permute-done.3, bf16[8,96,128]{2,1,0:T(8,128)(2,1)S(1)} %collective-permute-done.2, bf16[8,96,128]{2,1,0:T(8,128)(2,1)S(1)} %pair_block.4, f32[128]{0:T(128)S(1)} %copy-done.1), kind=kLoop, calls=%fused_computation | loop fusion | flops 983040 | bytes 983552 | tf_op jit(solution)/shard_map/convert_element_type | solution.py:131
Async XLA Ops:
  0.0 25.0 %copy-start = (bf16[128,96,32]{0,2,1:T(8,128)(2,1)S(1)}, bf16[128,96,32]{0,2,1:T(8,128)(2,1)}, u32[]{:S(2)}) copy-start(bf16[128,96,32]{0,2,1:T(8,128)(2,1)} %param.5) | copy-start | bytes 2359300
  1.7 19.2 %all-to-all-start = ((bf16[32,2,32,128]{3,2,1,0:T(8,128)(2,1)}), bf16[32,2,32,128]{3,2,1,0:T(8,128)(2,1)S(1)}, u32[]{:S(2)}, u32[]{:S(2)}) async-start(bf16[32,2,32,128]{3,2,1,0:T(8,128)(2,1)} %broadcast_in_dim.2), calls=%async_computation | async-start | bytes 1048576 | tf_op jit(solution)/shard_map/all_to_all | solution.py:113
  10.9 14.1 %collective-permute-start.1 = (bf16[96,32,128]{2,1,0:T(8,128)(2,1)}, bf16[96,32,128]{2,1,0:T(8,128)(2,1)S(1)}, u32[]{:S(2)}, u32[]{:S(2)}) collective-permute-start(bf16[96,32,128]{2,1,0:T(8,128)(2,1)} %bitcast.15), channel_id=1, source_target_pairs={{0,32},{32,0},{1,33},{33,1},{2,34},{34,2},{3,35},{35,3},{4,36},{36... | collective-permute-start | bytes 2359304 | tf_op jit(solution)/shard_map/ppermute | solution.py:111
  20.9 6.6 %collective-permute-start = (bf16[4,2,8,32,128]{4,3,2,1,0:T(8,128)(2,1)S(1)}, bf16[4,2,8,32,128]{4,3,2,1,0:T(8,128)(2,1)S(1)}, u32[]{:S(2)}, u32[]{:S(2)}) collective-permute-start(bf16[4,2,8,32,128]{4,3,2,1,0:T(8,128)(2,1)S(1)} %bitcast.18), channel_id=1, source_target_pairs={{0,32},{32,0},{1,33},{33,1},{2,34},{34,2},{3,35},{35,3},{4,36},{36... | collective-permute-start | bytes 1572872 | tf_op jit(solution)/shard_map/ppermute | solution.py:115
  29.5 16.0 %collective-permute-start.2 = (bf16[8,96,128]{2,1,0:T(8,128)(2,1)S(1)}, bf16[8,96,128]{2,1,0:T(8,128)(2,1)S(1)}, u32[]{:S(2)}, u32[]{:S(2)}) collective-permute-start(bf16[8,96,128]{2,1,0:T(8,128)(2,1)S(1)} %pair_block.5), channel_id=1, source_target_pairs={{0,128},{64,192},{128,0},{192,64},{1,129},{65,193},{129,1},{193,65... | collective-permute-start | bytes 589832 | tf_op jit(solution)/shard_map/ppermute | solution.py:127
  37.6 12.2 %collective-permute-start.3 = (bf16[8,96,128]{2,1,0:T(8,128)(2,1)S(1)}, bf16[8,96,128]{2,1,0:T(8,128)(2,1)S(1)}, u32[]{:S(2)}, u32[]{:S(2)}) collective-permute-start(bf16[8,96,128]{2,1,0:T(8,128)(2,1)S(1)} %pair_block.6), channel_id=1, source_target_pairs={{0,64},{64,128},{128,192},{192,0},{1,65},{65,129},{129,193},{193,1... | collective-permute-start | bytes 589832 | tf_op jit(solution)/shard_map/ppermute | solution.py:127
  40.9 13.1 %copy-start.1 = (f32[128]{0:T(128)S(1)}, f32[128]{0:T(128)}, u32[]{:S(2)}) copy-start(f32[128]{0:T(128)} %param.7) | copy-start | bytes 1540
  40.9 13.1 %collective-permute-start.4 = (bf16[8,96,128]{2,1,0:T(8,128)(2,1)S(1)}, bf16[8,96,128]{2,1,0:T(8,128)(2,1)S(1)}, u32[]{:S(2)}, u32[]{:S(2)}) collective-permute-start(bf16[8,96,128]{2,1,0:T(8,128)(2,1)S(1)} %pair_block.7), channel_id=1, source_target_pairs={{0,192},{64,0},{128,64},{192,128},{1,193},{65,1},{129,65},{193,129... | collective-permute-start | bytes 589832 | tf_op jit(solution)/shard_map/ppermute | solution.py:127

commit v2 on v0

v2 whole, which is shorter than its diff:
```python
import functools

import jax
import jax.numpy as jnp
from jax import lax
from jax.experimental import pallas as pl
from jax.experimental.pallas import tpu as pltpu
from jax.sharding import Mesh, PartitionSpec as P

FEATS = 32
ROWS = 8
LANES = 128
RING = 4
TILES = 32
DEPTH_AXES = ("zh", "core")
TILE_AXES = ("zl", "y", "x")
SWAP = [(0, 1), (1, 0)]
WHOLE = pl.BlockSpec(memory_space=pltpu.VMEM)
ANY = pl.BlockSpec(memory_space=pltpu.HBM)


def limit(mib):
    return pltpu.CompilerParams(vmem_limit_bytes=mib << 20)


def cost(nbytes, flops=0):
    return pl.CostEstimate(flops=flops, bytes_accessed=nbytes, transcendentals=0)


def spread_kernel(in_ref, out_ref, held_ref, filled_ref, in_sem, out_sem):
    fetch = pltpu.make_async_copy(in_ref, held_ref, in_sem)
    fetch.start()
    fetch.wait()
    own = held_ref[...]
    for t in range(TILES):
        filled_ref[t] = own
    store = pltpu.make_async_copy(filled_ref, out_ref, out_sem)
    store.start()
    store.wait()


def spread(own):
    return pl.pallas_call(
        spread_kernel,
        out_shape=jax.ShapeDtypeStruct((TILES,) + own.shape, jnp.bfloat16),
        in_specs=[ANY],
        out_specs=ANY,
        scratch_shapes=[
            pltpu.VMEM(own.shape, jnp.bfloat16),
            pltpu.VMEM((TILES,) + own.shape, jnp.bfloat16),
            pltpu.SemaphoreType.DMA,
            pltpu.SemaphoreType.DMA,
        ],
        compiler_params=limit(60),
        cost_estimate=cost(1 << 20),
        name="spread",
    )(own)


def turn(ref, wide_ref, out_ref):
    cols = ref.shape[0] // FEATS
    pad = jnp.zeros((LANES - cols, LANES), jnp.float32)
    wide_ref[...] = ref[...].astype(jnp.float32)
    for f in range(FEATS):
        picked = jnp.concatenate([wide_ref[pl.ds(f, cols, stride=FEATS), :], pad], axis=0)
        out_ref[0:LANES, f * LANES:(f + 1) * LANES] = picked.T.astype(jnp.bfloat16)


def own_kernel(b_ref, matrix_ref, out_ref, wide_ref, matrix_wide_ref, matrix_held_ref, sem):
    fetch = pltpu.make_async_copy(matrix_ref, matrix_held_ref, sem)
    fetch.start()
    turn(b_ref, wide_ref, out_ref)
    fetch.wait()
    matrix_wide_ref[...] = matrix_held_ref[...].astype(jnp.float32)
    group = LANES // FEATS
    for g in range(FEATS // group):
        rows = [
            matrix_wide_ref[pl.ds(g * group + i, FEATS, stride=FEATS), :] for i in range(group)
        ]
        out_ref[LANES:, g * LANES:(g + 1) * LANES] = jnp.concatenate(rows, axis=0).T.astype(
            jnp.bfloat16
        )


def turn_own(b, matrix):
    wide = (b.shape[0] * FEATS, LANES)
    return pl.pallas_call(
        own_kernel,
        out_shape=jax.ShapeDtypeStruct((2 * LANES, FEATS * LANES), jnp.bfloat16),
        scratch_shapes=[
            pltpu.VMEM(wide, jnp.float32),
            pltpu.VMEM(matrix.shape, jnp.float32),
            pltpu.VMEM(matrix.shape, jnp.bfloat16),
            pltpu.SemaphoreType.DMA,
        ],
        in_specs=[WHOLE, ANY],
        out_specs=WHOLE,
        compiler_params=limit(8),
        cost_estimate=cost(4 << 20),
        name="turn_own",
    )(b.reshape(wide), matrix)


def other_kernel(b_ref, out_ref, wide_ref):
    turn(b_ref, wide_ref, out_ref)


def turn_other(b):
    wide = (b.shape[0] * FEATS, LANES)
    return pl.pallas_call(
        other_kernel,
        out_shape=jax.ShapeDtypeStruct((LANES, FEATS * LANES), jnp.bfloat16),
        scratch_shapes=[pltpu.VMEM(wide, jnp.float32)],
        in_specs=[WHOLE],
        out_specs=WHOLE,
        compiler_params=limit(8),
        cost_estimate=cost(4 << 20),
        name="turn_other",
    )(b.reshape(wide))


def pair_kernel(hops, groups, own_ref, other_ref, b_own_ref, b_other_ref, out_ref, stack_ref):
    zh = lax.axis_index("zh")
    core = lax.axis_index("core")
    block = (zh + jnp.where(core == 0, hops[0], hops[1])) & (RING - 1)
    width = ROWS * FEATS
    parts = []
    for g in range(groups):
        half = core if g == 0 else 1 - core
        parts.append(
            jnp.concatenate(
                [
                    own_ref[block, half].reshape(width, LANES),
                    other_ref[block, half].reshape(width, LANES),
                ],
                axis=1,
            )
        )
    a = parts[0] if groups == 1 else jnp.concatenate(parts, axis=0)
    rows = ROWS * groups
    feats = 4
    for c in range(FEATS // feats):
        lanes = slice(c * feats * LANES, (c + 1) * feats * LANES)
        b = jnp.concatenate([b_own_ref[0:LANES, lanes], b_other_ref[:, lanes]], axis=0)
        outer = jnp.dot(a, b, preferred_element_type=jnp.float32).astype(jnp.bfloat16)
        for f in range(feats):
            k = (c * feats + f) * FEATS
            for r in range(rows):
                stack_ref[k:k + FEATS, r * LANES:(r + 1) * LANES] = outer[
                    r * FEATS:(r + 1) * FEATS, f * LANES:(f + 1) * LANES
                ]
    cols = out_ref.shape[1]
    w = b_own_ref[LANES:, 0:FEATS * FEATS]
    for r in range(0, rows, 2):
        mixed = jnp.dot(
            w, stack_ref[:, r * LANES:(r + 2) * LANES], preferred_element_type=jnp.float32
        )
        out_ref[r] = mixed[:, :LANES].T[:cols].astype(jnp.bfloat16)
        out_ref[r + 1] = mixed[:, LANES:].T[:cols].astype(jnp.bfloat16)


def pair_block(hops, groups, own, other, b_own, b_other, cols, flops=3 << 30):
    rows = ROWS * groups
    return pl.pallas_call(
        functools.partial(pair_kernel, hops, groups),
        out_shape=jax.ShapeDtypeStruct((rows, cols, LANES), jnp.bfloat16),
        in_specs=[WHOLE] * 4,
        out_specs=WHOLE,
        scratch_shapes=[pltpu.VMEM((FEATS * FEATS, rows * LANES), jnp.bfloat16)],
        compiler_params=limit(16),
        cost_estimate=cost(4 << 20, flops),
        name="pair_block",
    )(own, other, b_own, b_other)


def send(part, hops):
    pairs = []
    for z in range(RING):
        for c in range(2):
            pairs.append((z * 2 + c, (z + hops[c]) % RING * 2 + c))
    return lax.ppermute(part, DEPTH_AXES, pairs)


def local(first, second, matrix, bias):
    sequences = first.shape[0] * 2 * RING
    at = jnp.transpose(first, (1, 2, 0))
    bt = jnp.transpose(second, (1, 2, 0))
    cols = bt.shape[0]
    copies = spread(at)
    b_swapped = lax.ppermute(bt, "core", SWAP)
    a_own = lax.all_to_all(copies, TILE_AXES, split_axis=0, concat_axis=0, tiled=True)
    a_own = a_own.reshape(RING, 2, ROWS, FEATS, LANES)
    b_own = turn_own(bt, matrix)
    b_other = turn_other(b_swapped)
    a_swap, _ = lax.optimization_barrier((a_own, b_other))
    a_other = lax.ppermute(a_swap, "core", SWAP)
    block = functools.partial(
        pair_block, own=a_own, other=a_other, b_own=b_own, b_other=b_other, cols=cols
    )
    received = [send(block(hops, 1), hops) for hops in ((1, 3), (2, 2), (3, 1))]
    kept = block((0, 0), 1)
    parts = [kept] + received
    total = sum(part.astype(jnp.float32) for part in parts)
    return (total * (1.0 / sequences) + bias).astype(jnp.bfloat16)


def solution(mesh):
    fine = Mesh(mesh.devices.reshape(RING, 2, 2, 4, 4), DEPTH_AXES + TILE_AXES)
    in_specs = (P(DEPTH_AXES, TILE_AXES, None), P(DEPTH_AXES, TILE_AXES, None), P(), P())
    out_specs = P(DEPTH_AXES, TILE_AXES, None)
    return jax.shard_map(local, mesh=fine, in_specs=in_specs, out_specs=out_specs, check_vma=False)
```

time: 421 us -> 49.9 us (0.12)
  the two profiles are of different devices: /device:TPU:38 before, /device:TPU:33 now
where the time goes in v2:
time: 49.9 us; the launch traced here: 49.2 us
  starting transfers between devices  20.2 us (40%)
  waiting for transfers between devices  19.2 us (38%)
  Pallas kernels  8.9 us (18%)
  other arithmetic  0.81 us (2%)
    ppermute x3, waiting for transfers between devices, send(): return lax.ppermute(part, DEPTH_AXES, pairs)  12.1 us
    ppermute x3, starting transfers between devices, send(): return lax.ppermute(part, DEPTH_AXES, pairs)  8.62 us
    all_to_all x1, starting transfers between devices, local(): lax.all_to_all(copies, TILE_AXES, split_axis=0, concat_axis=0, tiled=True)  8.01 us
    all_to_all x1, waiting for transfers between devices, local(): lax.all_to_all(copies, TILE_AXES, split_axis=0, concat_axis=0, tiled=True)  5.01 us
    pallas_call x4, Pallas kernels, pair_block(): pl.pallas_call(functools.partial(pair_kernel, hops, groups), out_shape=ja...  4.5 us
    ppermute x1, starting transfers between devices, local(): a_other = lax.ppermute(a_swap, 'core', SWAP)  2.3 us
    ppermute x1, waiting for transfers between devices, local(): b_swapped = lax.ppermute(bt, 'core', SWAP)  2.12 us
    pallas_call x1, Pallas kernels, spread(): pl.pallas_call(spread_kernel, out_shape=jax.ShapeDtypeStruct((TILES,) + o...  1.74 us
  transfers between devices with their start and end apart: 6, of which 4 were waited for; matrix products, arithmetic and copies ran while one was open for 0% of the time, Pallas kernels for 12%

profile of v2, /device:TPU:33, one launch (start us, length us, event | category | flops | bytes accessed | tf_op | source)
XLA Modules:
  0.0 49.2 jit_solution(5674800061414644184)
XLA Ops:
  0.0 0.0 copy-start
  0.0 0.0 copy-start.1
  0.0 1.7 %spread.1 = bf16[32,2,32,128]{3,2,1,0:T(8,128)(2,1)} custom-call(bf16[2,32,128]{2,1,0:T(8,128)(2,1)} %bitcast.14), custom_call_target="tpu_custom_call" | custom-call | bytes 1048576 | tf_op jit(solution)/shard_map/spread/pallas_call | solution.py:43
  1.7 8.0 %all-to-all-start = ((bf16[32,2,32,128]{3,2,1,0:T(8,128)(2,1)}), bf16[32,2,32,128]{3,2,1,0:T(8,128)(2,1)S(1)}, u32[]{:S(2)}, u32[]{:S(2)}) async-start(bf16[32,2,32,128]{3,2,1,0:T(8,128)(2,1)} %spread.1), calls=%async_computation | async-start | bytes 1048576 | tf_op jit(solution)/shard_map/all_to_all | solution.py:191
  9.8 1.3 %collective-permute-start = (bf16[96,32,128]{2,1,0:T(8,128)(2,1)}, bf16[96,32,128]{2,1,0:T(8,128)(2,1)S(1)}, u32[]{:S(2)}, u32[]{:S(2)}) collective-permute-start(bf16[96,32,128]{2,1,0:T(8,128)(2,1)} %bitcast.7), channel_id=1, source_target_pairs={{0,32},{32,0},{1,33},{33,1},{2,34},{34,2},{3,35},{35,3},{4,36},{36... | collective-permute-start | bytes 2359304 | tf_op jit(solution)/shard_map/ppermute | solution.py:190
  11.1 2.1 %collective-permute-done = bf16[96,32,128]{2,1,0:T(8,128)(2,1)S(1)} collective-permute-done((bf16[96,32,128]{2,1,0:T(8,128)(2,1)}, bf16[96,32,128]{2,1,0:T(8,128)(2,1)S(1)}, u32[]{:S(2)}, u32[]{:S(2)}) %collective-permute-start) | collective-permute-done | bytes 786464 | tf_op jit(solution)/shard_map/ppermute | solution.py:190
  13.2 1.1 %turn_other.1.b_other_ref = bf16[128,4096]{1,0:T(8,128)(2,1)S(1)} custom-call(bf16[3072,128]{1,0:T(8,128)(2,1)S(1)} %bitcast.6), custom_call_target="tpu_custom_call" | custom-call | bytes 4194304 | tf_op jit(solution)/shard_map/turn_other/pallas_call | solution.py:110
  14.3 5.0 %all-to-all-done = bf16[32,2,32,128]{3,2,1,0:T(8,128)(2,1)S(1)} async-done(((bf16[32,2,32,128]{3,2,1,0:T(8,128)(2,1)}), bf16[32,2,32,128]{3,2,1,0:T(8,128)(2,1)S(1)}, u32[]{:S(2)}, u32[]{:S(2)}) %all-to-all-start) | async-done | bytes 524320 | tf_op jit(solution)/shard_map/all_to_all | solution.py:191
  19.3 2.3 %collective-permute-start.1 = (bf16[4,2,8,32,128]{4,3,2,1,0:T(8,128)(2,1)S(1)}, bf16[4,2,8,32,128]{4,3,2,1,0:T(8,128)(2,1)S(1)}, u32[]{:S(2)}, u32[]{:S(2)}) collective-permute-start(bf16[4,2,8,32,128]{4,3,2,1,0:T(8,128)(2,1)S(1)} %bitcast.9), channel_id=1, source_target_pairs={{0,32},{32,0},{1,33},{33,1},{2,34},{34,2},{3,35},{35,3},{4,36},{36... | collective-permute-start | bytes 1572872 | tf_op jit(solution)/shard_map/ppermute | solution.py:196
  21.6 0.0 copy-done
  21.6 0.0 copy-done.1
  21.6 1.6 %turn_own.1.b_own_ref = bf16[256,4096]{1,0:T(8,128)(2,1)S(1)} custom-call(bf16[3072,128]{1,0:T(8,128)(2,1)S(1)} %bitcast.8, bf16[1024,128]{1,0:T(8,128)(2,1)S(1)} %copy-done.1), custom_call_target="tpu_custom_call" | custom-call | bytes 4194304 | tf_op jit(solution)/shard_map/turn_own/pallas_call | solution.py:87
  23.2 0.0 collective-permute-done.1.other_ref
  23.2 1.1 %pair_block.5 = bf16[8,96,128]{2,1,0:T(8,128)(2,1)S(1)} custom-call(bf16[4,2,8,32,128]{4,3,2,1,0:T(8,128)(2,1)S(1)} %bitcast.10, bf16[4,2,8,32,128]{4,3,2,1,0:T(8,128)(2,1)S(1)} %collective-permute-done.1.other_ref, bf16[256,4096]{1,0:T(8,128)(2,1)S(1)} %turn_own.1.b_own_ref, bf16[128,4096]{1,0:T(8,128)(2,1)S(1)} %turn_other.1.b_other_ref), custom_call_target="tpu_custom_call" | custom-call | flops 3221225472 | bytes 4194304 | tf_op jit(solution)/shard_map/pair_block/pallas_call | solution.py:164
  24.3 5.2 %collective-permute-start.2 = (bf16[8,96,128]{2,1,0:T(8,128)(2,1)S(1)}, bf16[8,96,128]{2,1,0:T(8,128)(2,1)S(1)}, u32[]{:S(2)}, u32[]{:S(2)}) collective-permute-start(bf16[8,96,128]{2,1,0:T(8,128)(2,1)S(1)} %pair_block.5), channel_id=1, source_target_pairs={{0,64},{32,224},{64,128},{96,32},{128,192},{160,96},{192,0},{224,1... | collective-permute-start | bytes 589832 | tf_op jit(solution)/shard_map/ppermute | solution.py:181
  29.5 1.1 %pair_block.6 = bf16[8,96,128]{2,1,0:T(8,128)(2,1)S(1)} custom-call(bf16[4,2,8,32,128]{4,3,2,1,0:T(8,128)(2,1)S(1)} %bitcast.11, bf16[4,2,8,32,128]{4,3,2,1,0:T(8,128)(2,1)S(1)} %collective-permute-done.1.other_ref, bf16[256,4096]{1,0:T(8,128)(2,1)S(1)} %turn_own.1.b_own_ref, bf16[128,4096]{1,0:T(8,128)(2,1)S(1)} %turn_other.1.b_other_ref), custom_call_target="tpu_custom_call" | custom-call | flops 3221225472 | bytes 4194304 | tf_op jit(solution)/shard_map/pair_block/pallas_call | solution.py:164
  30.7 1.2 %collective-permute-start.3 = (bf16[8,96,128]{2,1,0:T(8,128)(2,1)S(1)}, bf16[8,96,128]{2,1,0:T(8,128)(2,1)S(1)}, u32[]{:S(2)}, u32[]{:S(2)}) collective-permute-start(bf16[8,96,128]{2,1,0:T(8,128)(2,1)S(1)} %pair_block.6), channel_id=1, source_target_pairs={{0,128},{32,160},{64,192},{96,224},{128,0},{160,32},{192,64},{224,... | collective-permute-start | bytes 589832 | tf_op jit(solution)/shard_map/ppermute | solution.py:181
  31.9 1.1 %pair_block.7 = bf16[8,96,128]{2,1,0:T(8,128)(2,1)S(1)} custom-call(bf16[4,2,8,32,128]{4,3,2,1,0:T(8,128)(2,1)S(1)} %bitcast.12, bf16[4,2,8,32,128]{4,3,2,1,0:T(8,128)(2,1)S(1)} %collective-permute-done.1.other_ref, bf16[256,4096]{1,0:T(8,128)(2,1)S(1)} %turn_own.1.b_own_ref, bf16[128,4096]{1,0:T(8,128)(2,1)S(1)} %turn_other.1.b_other_ref), custom_call_target="tpu_custom_call" | custom-call | flops 3221225472 | bytes 4194304 | tf_op jit(solution)/shard_map/pair_block/pallas_call | solution.py:164
  33.1 0.0 copy-start.2
  33.1 2.2 %collective-permute-start.4 = (bf16[8,96,128]{2,1,0:T(8,128)(2,1)S(1)}, bf16[8,96,128]{2,1,0:T(8,128)(2,1)S(1)}, u32[]{:S(2)}, u32[]{:S(2)}) collective-permute-start(bf16[8,96,128]{2,1,0:T(8,128)(2,1)S(1)} %pair_block.7), channel_id=1, source_target_pairs={{0,192},{32,96},{64,0},{96,160},{128,64},{160,224},{192,128},{224,... | collective-permute-start | bytes 589832 | tf_op jit(solution)/shard_map/ppermute | solution.py:181
  35.2 1.1 %pair_block.4 = bf16[8,96,128]{2,1,0:T(8,128)(2,1)S(1)} custom-call(bf16[4,2,8,32,128]{4,3,2,1,0:T(8,128)(2,1)S(1)} %bitcast.13, bf16[4,2,8,32,128]{4,3,2,1,0:T(8,128)(2,1)S(1)} %collective-permute-done.1.other_ref, bf16[256,4096]{1,0:T(8,128)(2,1)S(1)} %turn_own.1.b_own_ref, bf16[128,4096]{1,0:T(8,128)(2,1)S(1)} %turn_other.1.b_other_ref), custom_call_target="tpu_custom_call" | custom-call | flops 3221225472 | bytes 4194304 | tf_op jit(solution)/shard_map/pair_block/pallas_call | solution.py:164
  36.4 0.0 collective-permute-done.2
  36.4 9.5 %collective-permute-done.3 = bf16[8,96,128]{2,1,0:T(8,128)(2,1)S(1)} collective-permute-done((bf16[8,96,128]{2,1,0:T(8,128)(2,1)S(1)}, bf16[8,96,128]{2,1,0:T(8,128)(2,1)S(1)}, u32[]{:S(2)}, u32[]{:S(2)}) %collective-permute-start.3) | collective-permute-done | bytes 196640 | tf_op jit(solution)/shard_map/ppermute | solution.py:181
  45.8 2.6 %collective-permute-done.4 = bf16[8,96,128]{2,1,0:T(8,128)(2,1)S(1)} collective-permute-done((bf16[8,96,128]{2,1,0:T(8,128)(2,1)S(1)}, bf16[8,96,128]{2,1,0:T(8,128)(2,1)S(1)}, u32[]{:S(2)}, u32[]{:S(2)}) %collective-permute-start.4) | collective-permute-done | bytes 196640 | tf_op jit(solution)/shard_map/ppermute | solution.py:181
  48.4 0.0 copy-done.2
  48.4 0.8 %add_convert_fusion = bf16[8,96,128]{2,1,0:T(8,128)(2,1)} fusion(bf16[8,96,128]{2,1,0:T(8,128)(2,1)S(1)} %collective-permute-done.4, bf16[8,96,128]{2,1,0:T(8,128)(2,1)S(1)} %collective-permute-done.3, bf16[8,96,128]{2,1,0:T(8,128)(2,1)S(1)} %collective-permute-done.2, bf16[8,96,128]{2,1,0:T(8,128)(2,1)S(1)} %pair_block.4, f32[128]{0:T(128)S(1)} %copy-done.2), kind=kLoop, calls=%fused_computation | loop fusion | flops 983040 | bytes 983552 | tf_op jit(solution)/shard_map/convert_element_type | solution.py:204
Async XLA Ops:
  0.0 21.6 %copy-start = (bf16[128,96,32]{0,2,1:T(8,128)(2,1)S(1)}, bf16[128,96,32]{0,2,1:T(8,128)(2,1)}, u32[]{:S(2)}) copy-start(bf16[128,96,32]{0,2,1:T(8,128)(2,1)} %param.5) | copy-start | bytes 2359300
  0.0 21.6 %copy-start.1 = (bf16[1024,128]{1,0:T(8,128)(2,1)S(1)}, bf16[1024,128]{1,0:T(8,128)(2,1)}, u32[]{:S(2)}) copy-start(bf16[1024,128]{1,0:T(8,128)(2,1)} %matrix_ref.1) | copy-start | bytes 786436
  1.7 17.6 %all-to-all-start = ((bf16[32,2,32,128]{3,2,1,0:T(8,128)(2,1)}), bf16[32,2,32,128]{3,2,1,0:T(8,128)(2,1)S(1)}, u32[]{:S(2)}, u32[]{:S(2)}) async-start(bf16[32,2,32,128]{3,2,1,0:T(8,128)(2,1)} %spread.1), calls=%async_computation | async-start | bytes 1048576 | tf_op jit(solution)/shard_map/all_to_all | solution.py:191
  9.8 3.4 %collective-permute-start = (bf16[96,32,128]{2,1,0:T(8,128)(2,1)}, bf16[96,32,128]{2,1,0:T(8,128)(2,1)S(1)}, u32[]{:S(2)}, u32[]{:S(2)}) collective-permute-start(bf16[96,32,128]{2,1,0:T(8,128)(2,1)} %bitcast.7), channel_id=1, source_target_pairs={{0,32},{32,0},{1,33},{33,1},{2,34},{34,2},{3,35},{35,3},{4,36},{36... | collective-permute-start | bytes 2359304 | tf_op jit(solution)/shard_map/ppermute | solution.py:190
  19.3 3.9 %collective-permute-start.1 = (bf16[4,2,8,32,128]{4,3,2,1,0:T(8,128)(2,1)S(1)}, bf16[4,2,8,32,128]{4,3,2,1,0:T(8,128)(2,1)S(1)}, u32[]{:S(2)}, u32[]{:S(2)}) collective-permute-start(bf16[4,2,8,32,128]{4,3,2,1,0:T(8,128)(2,1)S(1)} %bitcast.9), channel_id=1, source_target_pairs={{0,32},{32,0},{1,33},{33,1},{2,34},{34,2},{3,35},{35,3},{4,36},{36... | collective-permute-start | bytes 1572872 | tf_op jit(solution)/shard_map/ppermute | solution.py:196
  24.3 12.0 %collective-permute-start.2 = (bf16[8,96,128]{2,1,0:T(8,128)(2,1)S(1)}, bf16[8,96,128]{2,1,0:T(8,128)(2,1)S(1)}, u32[]{:S(2)}, u32[]{:S(2)}) collective-permute-start(bf16[8,96,128]{2,1,0:T(8,128)(2,1)S(1)} %pair_block.5), channel_id=1, source_target_pairs={{0,64},{32,224},{64,128},{96,32},{128,192},{160,96},{192,0},{224,1... | collective-permute-start | bytes 589832 | tf_op jit(solution)/shard_map/ppermute | solution.py:181
  30.7 15.2 %collective-permute-start.3 = (bf16[8,96,128]{2,1,0:T(8,128)(2,1)S(1)}, bf16[8,96,128]{2,1,0:T(8,128)(2,1)S(1)}, u32[]{:S(2)}, u32[]{:S(2)}) collective-permute-start(bf16[8,96,128]{2,1,0:T(8,128)(2,1)S(1)} %pair_block.6), channel_id=1, source_target_pairs={{0,128},{32,160},{64,192},{96,224},{128,0},{160,32},{192,64},{224,... | collective-permute-start | bytes 589832 | tf_op jit(solution)/shard_map/ppermute | solution.py:181
  33.1 15.4 %copy-start.2 = (f32[128]{0:T(128)S(1)}, f32[128]{0:T(128)}, u32[]{:S(2)}) copy-start(f32[128]{0:T(128)} %param.7) | copy-start | bytes 1540
  33.1 15.4 %collective-permute-start.4 = (bf16[8,96,128]{2,1,0:T(8,128)(2,1)S(1)}, bf16[8,96,128]{2,1,0:T(8,128)(2,1)S(1)}, u32[]{:S(2)}, u32[]{:S(2)}) collective-permute-start(bf16[8,96,128]{2,1,0:T(8,128)(2,1)S(1)} %pair_block.7), channel_id=1, source_target_pairs={{0,192},{32,96},{64,0},{96,160},{128,64},{160,224},{192,128},{224,... | collective-permute-start | bytes 589832 | tf_op jit(solution)/shard_map/ppermute | solution.py:181

commit v3 on v2

--- a/solution.py
+++ b/solution.py
@@ -155,22 +155,38 @@
         mixed = jnp.dot(
             w, stack_ref[:, r * LANES:(r + 2) * LANES], preferred_element_type=jnp.float32
         )
-        out_ref[r] = mixed[:, :LANES].T[:cols].astype(jnp.bfloat16)
-        out_ref[r + 1] = mixed[:, LANES:].T[:cols].astype(jnp.bfloat16)
-
-
-def pair_block(hops, groups, own, other, b_own, b_other, cols, flops=3 << 30):
+        out_ref[r] = mixed[:, :LANES].T[:cols].astype(out_ref.dtype)
+        out_ref[r + 1] = mixed[:, LANES:].T[:cols].astype(out_ref.dtype)
+
+
+def pair_block(hops, groups, own, other, b_own, b_other, cols, dtype=jnp.bfloat16):
     rows = ROWS * groups
     return pl.pallas_call(
         functools.partial(pair_kernel, hops, groups),
-        out_shape=jax.ShapeDtypeStruct((rows, cols, LANES), jnp.bfloat16),
+        out_shape=jax.ShapeDtypeStruct((rows, cols, LANES), dtype),
         in_specs=[WHOLE] * 4,
         out_specs=WHOLE,
         scratch_shapes=[pltpu.VMEM((FEATS * FEATS, rows * LANES), jnp.bfloat16)],
         compiler_params=limit(16),
-        cost_estimate=cost(4 << 20, flops),
+        cost_estimate=cost(4 << 20, 3 << 30),
         name="pair_block",
     )(own, other, b_own, b_other)
+
+
+def add_kernel(kept_ref, came_ref, out_ref):
+    out_ref[...] = (kept_ref[...] + came_ref[...].astype(jnp.float32)).astype(out_ref.dtype)
+
+
+def add_to(kept, came, dtype, name):
+    return pl.pallas_call(
+        add_kernel,
+        out_shape=jax.ShapeDtypeStruct(kept.shape, dtype),
+        in_specs=[WHOLE, WHOLE],
+        out_specs=WHOLE,
+        compiler_params=limit(8),
+        cost_estimate=cost(200 << 20),
+        name=name,
+    )(kept, came)
 
 
 def send(part, hops):
@@ -197,10 +213,13 @@
     block = functools.partial(
         pair_block, own=a_own, other=a_other, b_own=b_own, b_other=b_other, cols=cols
     )
-    received = [send(block(hops, 1), hops) for hops in ((1, 3), (2, 2), (3, 1))]
-    kept = block((0, 0), 1)
-    parts = [kept] + received
-    total = sum(part.astype(jnp.float32) for part in parts)
+    far = send(block((2, 2), 1), (1, 3))
+    right = send(block((3, 1), 1), (3, 1))
+    left_part = block((1, 3), 1, dtype=jnp.float32)
+    kept = block((0, 0), 1, dtype=jnp.float32)
+    far, kept, left_part = lax.optimization_barrier((far, kept, left_part))
+    left = send(add_to(left_part, far, jnp.bfloat16, "merge"), (1, 3))
+    total = add_to(kept, right, jnp.float32, "presum") + left.astype(jnp.float32)
     return (total * (1.0 / sequences) + bias).astype(jnp.bfloat16)
 
 

time: 49.9 us -> 47.6 us (0.954)
  waiting for transfers between devices: 19.2 us -> 15.8 us
  starting transfers between devices: 20.2 us -> 21.4 us
    ppermute x3, waiting for transfers between devices: 12.1 us -> 8.67 us  [send(): return lax.ppermute(part, DEPTH_AXES, pairs)]
    ppermute x3, starting transfers between devices: 8.62 us -> 9.81 us  [send(): return lax.ppermute(part, DEPTH_AXES, pairs)]
  transfers between devices with their start and end apart: 6 -> 6, of which waited for: 4 -> 4; matrix products, arithmetic and copies ran while one was open for 0% -> 0% of each run, Pallas kernels for 12% -> 13%
where the time goes in v3:
time: 47.6 us; the launch traced here: 47.3 us
  starting transfers between devices  21.4 us (45%)
  waiting for transfers between devices  15.8 us (33%)
  Pallas kernels  9.15 us (19%)
  other arithmetic  0.74 us (2%)
    ppermute x3, starting transfers between devices, send(): return lax.ppermute(part, DEPTH_AXES, pairs)  9.81 us
    ppermute x3, waiting for transfers between devices, send(): return lax.ppermute(part, DEPTH_AXES, pairs)  8.67 us
    all_to_all x1, starting transfers between devices, local(): lax.all_to_all(copies, TILE_AXES, split_axis=0, concat_axis=0, tiled=True)  8.01 us
    all_to_all x1, waiting for transfers between devices, local(): lax.all_to_all(copies, TILE_AXES, split_axis=0, concat_axis=0, tiled=True)  5.01 us
    pallas_call x4, Pallas kernels, pair_block(): pl.pallas_call(functools.partial(pair_kernel, hops, groups), out_shape=ja...  4.68 us
    ppermute x1, starting transfers between devices, local(): a_other = lax.ppermute(a_swap, 'core', SWAP)  2.3 us
    ppermute x1, waiting for transfers between devices, local(): b_swapped = lax.ppermute(bt, 'core', SWAP)  2.12 us
    pallas_call x1, Pallas kernels, spread(): pl.pallas_call(spread_kernel, out_shape=jax.ShapeDtypeStruct((TILES,) + o...  1.74 us
  transfers between devices with their start and end apart: 6, of which 4 were waited for; matrix products, arithmetic and copies ran while one was open for 0% of the time, Pallas kernels for 13%

profile of v3, /device:TPU:33, one launch (start us, length us, event | category | flops | bytes accessed | tf_op | source)
XLA Modules:
  0.0 47.3 jit_solution(18387234135288230823)
XLA Ops:
  0.0 0.0 copy-start
  0.0 0.0 copy-start.1
  0.0 1.7 %spread.1 = bf16[32,2,32,128]{3,2,1,0:T(8,128)(2,1)} custom-call(bf16[2,32,128]{2,1,0:T(8,128)(2,1)} %bitcast.14), custom_call_target="tpu_custom_call" | custom-call | bytes 1048576 | tf_op jit(solution)/shard_map/spread/pallas_call | solution.py:43
  1.7 8.0 %all-to-all-start = ((bf16[32,2,32,128]{3,2,1,0:T(8,128)(2,1)}), bf16[32,2,32,128]{3,2,1,0:T(8,128)(2,1)S(1)}, u32[]{:S(2)}, u32[]{:S(2)}) async-start(bf16[32,2,32,128]{3,2,1,0:T(8,128)(2,1)} %spread.1), calls=%async_computation | async-start | bytes 1048576 | tf_op jit(solution)/shard_map/all_to_all | solution.py:207
  9.8 1.3 %collective-permute-start = (bf16[96,32,128]{2,1,0:T(8,128)(2,1)}, bf16[96,32,128]{2,1,0:T(8,128)(2,1)S(1)}, u32[]{:S(2)}, u32[]{:S(2)}) collective-permute-start(bf16[96,32,128]{2,1,0:T(8,128)(2,1)} %bitcast.7), channel_id=1, source_target_pairs={{0,32},{32,0},{1,33},{33,1},{2,34},{34,2},{3,35},{35,3},{4,36},{36... | collective-permute-start | bytes 2359304 | tf_op jit(solution)/shard_map/ppermute | solution.py:206
  11.1 2.1 %collective-permute-done = bf16[96,32,128]{2,1,0:T(8,128)(2,1)S(1)} collective-permute-done((bf16[96,32,128]{2,1,0:T(8,128)(2,1)}, bf16[96,32,128]{2,1,0:T(8,128)(2,1)S(1)}, u32[]{:S(2)}, u32[]{:S(2)}) %collective-permute-start) | collective-permute-done | bytes 786464 | tf_op jit(solution)/shard_map/ppermute | solution.py:206
  13.2 1.1 %turn_other.1.b_other_ref = bf16[128,4096]{1,0:T(8,128)(2,1)S(1)} custom-call(bf16[3072,128]{1,0:T(8,128)(2,1)S(1)} %bitcast.6), custom_call_target="tpu_custom_call" | custom-call | bytes 4194304 | tf_op jit(solution)/shard_map/turn_other/pallas_call | solution.py:110
  14.3 5.0 %all-to-all-done = bf16[32,2,32,128]{3,2,1,0:T(8,128)(2,1)S(1)} async-done(((bf16[32,2,32,128]{3,2,1,0:T(8,128)(2,1)}), bf16[32,2,32,128]{3,2,1,0:T(8,128)(2,1)S(1)}, u32[]{:S(2)}, u32[]{:S(2)}) %all-to-all-start) | async-done | bytes 524320 | tf_op jit(solution)/shard_map/all_to_all | solution.py:207
  19.3 2.3 %collective-permute-start.1 = (bf16[4,2,8,32,128]{4,3,2,1,0:T(8,128)(2,1)S(1)}, bf16[4,2,8,32,128]{4,3,2,1,0:T(8,128)(2,1)S(1)}, u32[]{:S(2)}, u32[]{:S(2)}) collective-permute-start(bf16[4,2,8,32,128]{4,3,2,1,0:T(8,128)(2,1)S(1)} %bitcast.9), channel_id=1, source_target_pairs={{0,32},{32,0},{1,33},{33,1},{2,34},{34,2},{3,35},{35,3},{4,36},{36... | collective-permute-start | bytes 1572872 | tf_op jit(solution)/shard_map/ppermute | solution.py:212
  21.6 0.0 copy-done
  21.6 0.0 copy-done.1
  21.6 1.6 %turn_own.1.b_own_ref = bf16[256,4096]{1,0:T(8,128)(2,1)S(1)} custom-call(bf16[3072,128]{1,0:T(8,128)(2,1)S(1)} %bitcast.8, bf16[1024,128]{1,0:T(8,128)(2,1)S(1)} %copy-done.1), custom_call_target="tpu_custom_call" | custom-call | bytes 4194304 | tf_op jit(solution)/shard_map/turn_own/pallas_call | solution.py:87
  23.2 0.0 collective-permute-done.1.other_ref
  23.2 1.1 %pair_block.4 = bf16[8,96,128]{2,1,0:T(8,128)(2,1)S(1)} custom-call(bf16[4,2,8,32,128]{4,3,2,1,0:T(8,128)(2,1)S(1)} %bitcast.10, bf16[4,2,8,32,128]{4,3,2,1,0:T(8,128)(2,1)S(1)} %collective-permute-done.1.other_ref, bf16[256,4096]{1,0:T(8,128)(2,1)S(1)} %turn_own.1.b_own_ref, bf16[128,4096]{1,0:T(8,128)(2,1)S(1)} %turn_other.1.b_other_ref), custom_call_target="tpu_custom_call" | custom-call | flops 3221225472 | bytes 4194304 | tf_op jit(solution)/shard_map/pair_block/pallas_call | solution.py:164
  24.3 5.2 %collective-permute-start.2 = (bf16[8,96,128]{2,1,0:T(8,128)(2,1)S(1)}, bf16[8,96,128]{2,1,0:T(8,128)(2,1)S(1)}, u32[]{:S(2)}, u32[]{:S(2)}) collective-permute-start(bf16[8,96,128]{2,1,0:T(8,128)(2,1)S(1)} %pair_block.4), channel_id=1, source_target_pairs={{0,64},{32,224},{64,128},{96,32},{128,192},{160,96},{192,0},{224,1... | collective-permute-start | bytes 589832 | tf_op jit(solution)/shard_map/ppermute | solution.py:197
  29.5 1.1 %pair_block.7 = bf16[8,96,128]{2,1,0:T(8,128)(2,1)S(1)} custom-call(bf16[4,2,8,32,128]{4,3,2,1,0:T(8,128)(2,1)S(1)} %bitcast.11, bf16[4,2,8,32,128]{4,3,2,1,0:T(8,128)(2,1)S(1)} %collective-permute-done.1.other_ref, bf16[256,4096]{1,0:T(8,128)(2,1)S(1)} %turn_own.1.b_own_ref, bf16[128,4096]{1,0:T(8,128)(2,1)S(1)} %turn_other.1.b_other_ref), custom_call_target="tpu_custom_call" | custom-call | flops 3221225472 | bytes 4194304 | tf_op jit(solution)/shard_map/pair_block/pallas_call | solution.py:164
  30.7 0.1 collective-permute-start.3
  30.8 1.2 %pair_block.6.kept_ref = f32[8,96,128]{2,1,0:T(8,128)S(1)} custom-call(bf16[4,2,8,32,128]{4,3,2,1,0:T(8,128)(2,1)S(1)} %bitcast.12, bf16[4,2,8,32,128]{4,3,2,1,0:T(8,128)(2,1)S(1)} %collective-permute-done.1.other_ref, bf16[256,4096]{1,0:T(8,128)(2,1)S(1)} %turn_own.1.b_own_ref, bf16[128,4096]{1,0:T(8,128)(2,1)S(1)} %turn_other.1.b_other_ref), custom_call_target="tpu_custom_call" | custom-call | flops 3221225472 | bytes 4194304 | tf_op jit(solution)/shard_map/pair_block/pallas_call | solution.py:164
  32.0 0.0 copy-start.2
  32.0 1.2 %pair_block.5.kept_ref = f32[8,96,128]{2,1,0:T(8,128)S(1)} custom-call(bf16[4,2,8,32,128]{4,3,2,1,0:T(8,128)(2,1)S(1)} %bitcast.13, bf16[4,2,8,32,128]{4,3,2,1,0:T(8,128)(2,1)S(1)} %collective-permute-done.1.other_ref, bf16[256,4096]{1,0:T(8,128)(2,1)S(1)} %turn_own.1.b_own_ref, bf16[128,4096]{1,0:T(8,128)(2,1)S(1)} %turn_other.1.b_other_ref), custom_call_target="tpu_custom_call" | custom-call | flops 3221225472 | bytes 4194304 | tf_op jit(solution)/shard_map/pair_block/pallas_call | solution.py:164
  33.2 6.1 %collective-permute-done.2.came_ref = bf16[8,96,128]{2,1,0:T(8,128)(2,1)S(1)} collective-permute-done((bf16[8,96,128]{2,1,0:T(8,128)(2,1)S(1)}, bf16[8,96,128]{2,1,0:T(8,128)(2,1)S(1)}, u32[]{:S(2)}, u32[]{:S(2)}) %collective-permute-start.2) | collective-permute-done | bytes 196640 | tf_op jit(solution)/shard_map/ppermute | solution.py:197
  39.4 4.5 %collective-permute-start.4 = (bf16[8,96,128]{2,1,0:T(8,128)(2,1)S(1)}, bf16[8,96,128]{2,1,0:T(8,128)(2,1)S(1)}, u32[]{:S(2)}, u32[]{:S(2)}) collective-permute-start(bf16[8,96,128]{2,1,0:T(8,128)(2,1)S(1)} %merge.1), channel_id=1, source_target_pairs={{0,64},{32,224},{64,128},{96,32},{128,192},{160,96},{192,0},{224,1... | collective-permute-start | bytes 589832 | tf_op jit(solution)/shard_map/ppermute | solution.py:197
  43.9 0.0 collective-permute-done.3.came_ref
  43.9 2.6 %collective-permute-done.4 = bf16[8,96,128]{2,1,0:T(8,128)(2,1)S(1)} collective-permute-done((bf16[8,96,128]{2,1,0:T(8,128)(2,1)S(1)}, bf16[8,96,128]{2,1,0:T(8,128)(2,1)S(1)}, u32[]{:S(2)}, u32[]{:S(2)}) %collective-permute-start.4) | collective-permute-done | bytes 196640 | tf_op jit(solution)/shard_map/ppermute | solution.py:197
  46.5 0.0 copy-done.2
  46.5 0.7 %add_convert_fusion = bf16[8,96,128]{2,1,0:T(8,128)(2,1)} fusion(f32[8,96,128]{2,1,0:T(8,128)S(1)} %presum.1, bf16[8,96,128]{2,1,0:T(8,128)(2,1)S(1)} %collective-permute-done.4, f32[128]{0:T(128)S(1)} %copy-done.2), kind=kLoop, calls=%fused_computation | loop fusion | flops 491520 | bytes 786944 | tf_op jit(solution)/shard_map/convert_element_type | solution.py:223
  (2 shorter events, 0.1 us)
Async XLA Ops:
  0.0 21.6 %copy-start = (bf16[128,96,32]{0,2,1:T(8,128)(2,1)S(1)}, bf16[128,96,32]{0,2,1:T(8,128)(2,1)}, u32[]{:S(2)}) copy-start(bf16[128,96,32]{0,2,1:T(8,128)(2,1)} %param.5) | copy-start | bytes 2359300
  0.0 21.6 %copy-start.1 = (bf16[1024,128]{1,0:T(8,128)(2,1)S(1)}, bf16[1024,128]{1,0:T(8,128)(2,1)}, u32[]{:S(2)}) copy-start(bf16[1024,128]{1,0:T(8,128)(2,1)} %matrix_ref.1) | copy-start | bytes 786436
  1.7 17.6 %all-to-all-start = ((bf16[32,2,32,128]{3,2,1,0:T(8,128)(2,1)}), bf16[32,2,32,128]{3,2,1,0:T(8,128)(2,1)S(1)}, u32[]{:S(2)}, u32[]{:S(2)}) async-start(bf16[32,2,32,128]{3,2,1,0:T(8,128)(2,1)} %spread.1), calls=%async_computation | async-start | bytes 1048576 | tf_op jit(solution)/shard_map/all_to_all | solution.py:207
  9.8 3.4 %collective-permute-start = (bf16[96,32,128]{2,1,0:T(8,128)(2,1)}, bf16[96,32,128]{2,1,0:T(8,128)(2,1)S(1)}, u32[]{:S(2)}, u32[]{:S(2)}) collective-permute-start(bf16[96,32,128]{2,1,0:T(8,128)(2,1)} %bitcast.7), channel_id=1, source_target_pairs={{0,32},{32,0},{1,33},{33,1},{2,34},{34,2},{3,35},{35,3},{4,36},{36... | collective-permute-start | bytes 2359304 | tf_op jit(solution)/shard_map/ppermute | solution.py:206
  19.3 3.9 %collective-permute-start.1 = (bf16[4,2,8,32,128]{4,3,2,1,0:T(8,128)(2,1)S(1)}, bf16[4,2,8,32,128]{4,3,2,1,0:T(8,128)(2,1)S(1)}, u32[]{:S(2)}, u32[]{:S(2)}) collective-permute-start(bf16[4,2,8,32,128]{4,3,2,1,0:T(8,128)(2,1)S(1)} %bitcast.9), channel_id=1, source_target_pairs={{0,32},{32,0},{1,33},{33,1},{2,34},{34,2},{3,35},{35,3},{4,36},{36... | collective-permute-start | bytes 1572872 | tf_op jit(solution)/shard_map/ppermute | solution.py:212
  24.3 15.0 %collective-permute-start.2 = (bf16[8,96,128]{2,1,0:T(8,128)(2,1)S(1)}, bf16[8,96,128]{2,1,0:T(8,128)(2,1)S(1)}, u32[]{:S(2)}, u32[]{:S(2)}) collective-permute-start(bf16[8,96,128]{2,1,0:T(8,128)(2,1)S(1)} %pair_block.4), channel_id=1, source_target_pairs={{0,64},{32,224},{64,128},{96,32},{128,192},{160,96},{192,0},{224,1... | collective-permute-start | bytes 589832 | tf_op jit(solution)/shard_map/ppermute | solution.py:197
  30.7 13.2 %collective-permute-start.3 = (bf16[8,96,128]{2,1,0:T(8,128)(2,1)S(1)}, bf16[8,96,128]{2,1,0:T(8,128)(2,1)S(1)}, u32[]{:S(2)}, u32[]{:S(2)}) collective-permute-start(bf16[8,96,128]{2,1,0:T(8,128)(2,1)S(1)} %pair_block.7), channel_id=1, source_target_pairs={{0,192},{32,96},{64,0},{96,160},{128,64},{160,224},{192,128},{224,... | collective-permute-start | bytes 589832 | tf_op jit(solution)/shard_map/ppermute | solution.py:197
  32.0 14.5 %copy-start.2 = (f32[128]{0:T(128)S(1)}, f32[128]{0:T(128)}, u32[]{:S(2)}) copy-start(f32[128]{0:T(128)} %param.7) | copy-start | bytes 1540
  39.4 7.1 %collective-permute-start.4 = (bf16[8,96,128]{2,1,0:T(8,128)(2,1)S(1)}, bf16[8,96,128]{2,1,0:T(8,128)(2,1)S(1)}, u32[]{:S(2)}, u32[]{:S(2)}) collective-permute-start(bf16[8,96,128]{2,1,0:T(8,128)(2,1)S(1)} %merge.1), channel_id=1, source_target_pairs={{0,64},{32,224},{64,128},{96,32},{128,192},{160,96},{192,0},{224,1... | collective-permute-start | bytes 589832 | tf_op jit(solution)/shard_map/ppermute | solution.py:197

commit v4 on v3

--- a/solution.py
+++ b/solution.py
@@ -119,25 +119,19 @@
     )(b.reshape(wide))
 
 
-def pair_kernel(hops, groups, own_ref, other_ref, b_own_ref, b_other_ref, out_ref, stack_ref):
+def pair_kernel(hops, flip, own_ref, other_ref, b_own_ref, b_other_ref, out_ref, stack_ref):
     zh = lax.axis_index("zh")
     core = lax.axis_index("core")
     block = (zh + jnp.where(core == 0, hops[0], hops[1])) & (RING - 1)
+    half = 1 - core if flip else core
     width = ROWS * FEATS
-    parts = []
-    for g in range(groups):
-        half = core if g == 0 else 1 - core
-        parts.append(
-            jnp.concatenate(
-                [
-                    own_ref[block, half].reshape(width, LANES),
-                    other_ref[block, half].reshape(width, LANES),
-                ],
-                axis=1,
-            )
-        )
-    a = parts[0] if groups == 1 else jnp.concatenate(parts, axis=0)
-    rows = ROWS * groups
+    a = jnp.concatenate(
+        [
+            own_ref[block, half].reshape(width, LANES),
+            other_ref[block, half].reshape(width, LANES),
+        ],
+        axis=1,
+    )
     feats = 4
     for c in range(FEATS // feats):
         lanes = slice(c * feats * LANES, (c + 1) * feats * LANES)
@@ -145,13 +139,13 @@
         outer = jnp.dot(a, b, preferred_element_type=jnp.float32).astype(jnp.bfloat16)
         for f in range(feats):
             k = (c * feats + f) * FEATS
-            for r in range(rows):
+            for r in range(ROWS):
                 stack_ref[k:k + FEATS, r * LANES:(r + 1) * LANES] = outer[
                     r * FEATS:(r + 1) * FEATS, f * LANES:(f + 1) * LANES
                 ]
     cols = out_ref.shape[1]
     w = b_own_ref[LANES:, 0:FEATS * FEATS]
-    for r in range(0, rows, 2):
+    for r in range(0, ROWS, 2):
         mixed = jnp.dot(
             w, stack_ref[:, r * LANES:(r + 2) * LANES], preferred_element_type=jnp.float32
         )
@@ -159,14 +153,13 @@
         out_ref[r + 1] = mixed[:, LANES:].T[:cols].astype(out_ref.dtype)
 
 
-def pair_block(hops, groups, own, other, b_own, b_other, cols, dtype=jnp.bfloat16):
-    rows = ROWS * groups
-    return pl.pallas_call(
-        functools.partial(pair_kernel, hops, groups),
-        out_shape=jax.ShapeDtypeStruct((rows, cols, LANES), dtype),
+def pair_block(hops, flip, own, other, b_own, b_other, cols, dtype=jnp.bfloat16):
+    return pl.pallas_call(
+        functools.partial(pair_kernel, hops, flip),
+        out_shape=jax.ShapeDtypeStruct((ROWS, cols, LANES), dtype),
         in_specs=[WHOLE] * 4,
         out_specs=WHOLE,
-        scratch_shapes=[pltpu.VMEM((FEATS * FEATS, rows * LANES), jnp.bfloat16)],
+        scratch_shapes=[pltpu.VMEM((FEATS * FEATS, ROWS * LANES), jnp.bfloat16)],
         compiler_params=limit(16),
         cost_estimate=cost(4 << 20, 3 << 30),
         name="pair_block",
@@ -177,23 +170,23 @@
     out_ref[...] = (kept_ref[...] + came_ref[...].astype(jnp.float32)).astype(out_ref.dtype)
 
 
-def add_to(kept, came, dtype, name):
+def add_to(kept, came, dtype, name, nbytes):
     return pl.pallas_call(
         add_kernel,
         out_shape=jax.ShapeDtypeStruct(kept.shape, dtype),
         in_specs=[WHOLE, WHOLE],
         out_specs=WHOLE,
         compiler_params=limit(8),
-        cost_estimate=cost(200 << 20),
+        cost_estimate=cost(nbytes),
         name=name,
     )(kept, came)
 
 
-def send(part, hops):
+def send(part, hops, flip=0):
     pairs = []
     for z in range(RING):
         for c in range(2):
-            pairs.append((z * 2 + c, (z + hops[c]) % RING * 2 + c))
+            pairs.append((z * 2 + c, (z + hops[c]) % RING * 2 + (c ^ flip)))
     return lax.ppermute(part, DEPTH_AXES, pairs)
 
 
@@ -213,13 +206,14 @@
     block = functools.partial(
         pair_block, own=a_own, other=a_other, b_own=b_own, b_other=b_other, cols=cols
     )
-    far = send(block((2, 2), 1), (1, 3))
-    right = send(block((3, 1), 1), (3, 1))
-    left_part = block((1, 3), 1, dtype=jnp.float32)
-    kept = block((0, 0), 1, dtype=jnp.float32)
+    far = send(block((2, 2), False), (1, 3))
+    left_part = block((1, 3), False, dtype=jnp.float32)
+    right = send(block((1, 3), True), (1, 3), 1)
+    kept = block((0, 0), False, dtype=jnp.float32)
     far, kept, left_part = lax.optimization_barrier((far, kept, left_part))
-    left = send(add_to(left_part, far, jnp.bfloat16, "merge"), (1, 3))
-    total = add_to(kept, right, jnp.float32, "presum") + left.astype(jnp.float32)
+    merged = add_to(left_part, far, jnp.bfloat16, "merge", 200 << 20)
+    left = send(merged, (1, 3))
+    total = add_to(kept, right, jnp.float32, "presum", 200 << 20) + left.astype(jnp.float32)
     return (total * (1.0 / sequences) + bias).astype(jnp.bfloat16)
 
 

time: 47.6 us -> 45.9 us (0.964); the launches traced: 47.3 us -> 45 us
  waiting for transfers between devices: 15.8 us -> 13.8 us
    ppermute x3, waiting for transfers between devices: 8.67 us -> 6.67 us  [send(): return lax.ppermute(part, DEPTH_AXES, pairs)]
  transfers between devices with their start and end apart: 6 -> 6, of which waited for: 4 -> 5; matrix products, arithmetic and copies ran while one was open for 0% -> 0% of each run, Pallas kernels for 13% -> 14%
where the time goes in v4:
time: 45.9 us; the launch traced here: 45 us
  starting transfers between devices  21.2 us (46%)
  waiting for transfers between devices  13.8 us (30%)
  Pallas kernels  9.15 us (20%)
  other arithmetic  0.74 us (2%)
    ppermute x3, starting transfers between devices, send(): return lax.ppermute(part, DEPTH_AXES, pairs)  9.61 us
    all_to_all x1, starting transfers between devices, local(): lax.all_to_all(copies, TILE_AXES, split_axis=0, concat_axis=0, tiled=True)  8.01 us
    ppermute x3, waiting for transfers between devices, send(): return lax.ppermute(part, DEPTH_AXES, pairs)  6.67 us
    all_to_all x1, waiting for transfers between devices, local(): lax.all_to_all(copies, TILE_AXES, split_axis=0, concat_axis=0, tiled=True)  5.01 us
    pallas_call x4, Pallas kernels, pair_block(): pl.pallas_call(functools.partial(pair_kernel, hops, flip), out_shape=jax....  4.68 us
    ppermute x1, starting transfers between devices, local(): a_other = lax.ppermute(a_swap, 'core', SWAP)  2.3 us
    ppermute x1, waiting for transfers between devices, local(): b_swapped = lax.ppermute(bt, 'core', SWAP)  2.12 us
    pallas_call x1, Pallas kernels, spread(): pl.pallas_call(spread_kernel, out_shape=jax.ShapeDtypeStruct((TILES,) + o...  1.74 us
  transfers between devices with their start and end apart: 6, of which 5 were waited for; matrix products, arithmetic and copies ran while one was open for 0% of the time, Pallas kernels for 14%

profile of v4, /device:TPU:33, one launch (start us, length us, event | category | flops | bytes accessed | tf_op | source)
XLA Modules:
  0.0 45.0 jit_solution(9823487674250730551)
XLA Ops:
  0.0 0.0 copy-start
  0.0 0.0 copy-start.1
  0.0 1.7 %spread.1 = bf16[32,2,32,128]{3,2,1,0:T(8,128)(2,1)} custom-call(bf16[2,32,128]{2,1,0:T(8,128)(2,1)} %bitcast.14), custom_call_target="tpu_custom_call" | custom-call | bytes 1048576 | tf_op jit(solution)/shard_map/spread/pallas_call | solution.py:43
  1.7 8.0 %all-to-all-start = ((bf16[32,2,32,128]{3,2,1,0:T(8,128)(2,1)}), bf16[32,2,32,128]{3,2,1,0:T(8,128)(2,1)S(1)}, u32[]{:S(2)}, u32[]{:S(2)}) async-start(bf16[32,2,32,128]{3,2,1,0:T(8,128)(2,1)} %spread.1), calls=%async_computation | async-start | bytes 1048576 | tf_op jit(solution)/shard_map/all_to_all | solution.py:200
  9.8 1.3 %collective-permute-start = (bf16[96,32,128]{2,1,0:T(8,128)(2,1)}, bf16[96,32,128]{2,1,0:T(8,128)(2,1)S(1)}, u32[]{:S(2)}, u32[]{:S(2)}) collective-permute-start(bf16[96,32,128]{2,1,0:T(8,128)(2,1)} %bitcast.7), channel_id=1, source_target_pairs={{0,32},{32,0},{1,33},{33,1},{2,34},{34,2},{3,35},{35,3},{4,36},{36... | collective-permute-start | bytes 2359304 | tf_op jit(solution)/shard_map/ppermute | solution.py:199
  11.1 2.1 %collective-permute-done = bf16[96,32,128]{2,1,0:T(8,128)(2,1)S(1)} collective-permute-done((bf16[96,32,128]{2,1,0:T(8,128)(2,1)}, bf16[96,32,128]{2,1,0:T(8,128)(2,1)S(1)}, u32[]{:S(2)}, u32[]{:S(2)}) %collective-permute-start) | collective-permute-done | bytes 786464 | tf_op jit(solution)/shard_map/ppermute | solution.py:199
  13.2 1.1 %turn_other.1.b_other_ref = bf16[128,4096]{1,0:T(8,128)(2,1)S(1)} custom-call(bf16[3072,128]{1,0:T(8,128)(2,1)S(1)} %bitcast.6), custom_call_target="tpu_custom_call" | custom-call | bytes 4194304 | tf_op jit(solution)/shard_map/turn_other/pallas_call | solution.py:110
  14.3 5.0 %all-to-all-done = bf16[32,2,32,128]{3,2,1,0:T(8,128)(2,1)S(1)} async-done(((bf16[32,2,32,128]{3,2,1,0:T(8,128)(2,1)}), bf16[32,2,32,128]{3,2,1,0:T(8,128)(2,1)S(1)}, u32[]{:S(2)}, u32[]{:S(2)}) %all-to-all-start) | async-done | bytes 524320 | tf_op jit(solution)/shard_map/all_to_all | solution.py:200
  19.3 2.3 %collective-permute-start.1 = (bf16[4,2,8,32,128]{4,3,2,1,0:T(8,128)(2,1)S(1)}, bf16[4,2,8,32,128]{4,3,2,1,0:T(8,128)(2,1)S(1)}, u32[]{:S(2)}, u32[]{:S(2)}) collective-permute-start(bf16[4,2,8,32,128]{4,3,2,1,0:T(8,128)(2,1)S(1)} %bitcast.9), channel_id=1, source_target_pairs={{0,32},{32,0},{1,33},{33,1},{2,34},{34,2},{3,35},{35,3},{4,36},{36... | collective-permute-start | bytes 1572872 | tf_op jit(solution)/shard_map/ppermute | solution.py:205
  21.6 0.0 copy-done
  21.6 0.0 copy-done.1
  21.6 1.6 %turn_own.1.b_own_ref = bf16[256,4096]{1,0:T(8,128)(2,1)S(1)} custom-call(bf16[3072,128]{1,0:T(8,128)(2,1)S(1)} %bitcast.8, bf16[1024,128]{1,0:T(8,128)(2,1)S(1)} %copy-done.1), custom_call_target="tpu_custom_call" | custom-call | bytes 4194304 | tf_op jit(solution)/shard_map/turn_own/pallas_call | solution.py:87
  23.2 0.0 collective-permute-done.1.other_ref
  23.2 1.1 %pair_block.4 = bf16[8,96,128]{2,1,0:T(8,128)(2,1)S(1)} custom-call(bf16[4,2,8,32,128]{4,3,2,1,0:T(8,128)(2,1)S(1)} %bitcast.10, bf16[4,2,8,32,128]{4,3,2,1,0:T(8,128)(2,1)S(1)} %collective-permute-done.1.other_ref, bf16[256,4096]{1,0:T(8,128)(2,1)S(1)} %turn_own.1.b_own_ref, bf16[128,4096]{1,0:T(8,128)(2,1)S(1)} %turn_other.1.b_other_ref), custom_call_target="tpu_custom_call" | custom-call | flops 3221225472 | bytes 4194304 | tf_op jit(solution)/shard_map/pair_block/pallas_call | solution.py:157
  24.3 5.2 %collective-permute-start.2 = (bf16[8,96,128]{2,1,0:T(8,128)(2,1)S(1)}, bf16[8,96,128]{2,1,0:T(8,128)(2,1)S(1)}, u32[]{:S(2)}, u32[]{:S(2)}) collective-permute-start(bf16[8,96,128]{2,1,0:T(8,128)(2,1)S(1)} %pair_block.4), channel_id=1, source_target_pairs={{0,64},{32,224},{64,128},{96,32},{128,192},{160,96},{192,0},{224,1... | collective-permute-start | bytes 589832 | tf_op jit(solution)/shard_map/ppermute | solution.py:190
  29.5 1.1 %pair_block.7 = bf16[8,96,128]{2,1,0:T(8,128)(2,1)S(1)} custom-call(bf16[4,2,8,32,128]{4,3,2,1,0:T(8,128)(2,1)S(1)} %bitcast.11, bf16[4,2,8,32,128]{4,3,2,1,0:T(8,128)(2,1)S(1)} %collective-permute-done.1.other_ref, bf16[256,4096]{1,0:T(8,128)(2,1)S(1)} %turn_own.1.b_own_ref, bf16[128,4096]{1,0:T(8,128)(2,1)S(1)} %turn_other.1.b_other_ref), custom_call_target="tpu_custom_call" | custom-call | flops 3221225472 | bytes 4194304 | tf_op jit(solution)/shard_map/pair_block/pallas_call | solution.py:157
  30.7 0.3 collective-permute-start.3
  31.0 1.2 %pair_block.6.kept_ref = f32[8,96,128]{2,1,0:T(8,128)S(1)} custom-call(bf16[4,2,8,32,128]{4,3,2,1,0:T(8,128)(2,1)S(1)} %bitcast.12, bf16[4,2,8,32,128]{4,3,2,1,0:T(8,128)(2,1)S(1)} %collective-permute-done.1.other_ref, bf16[256,4096]{1,0:T(8,128)(2,1)S(1)} %turn_own.1.b_own_ref, bf16[128,4096]{1,0:T(8,128)(2,1)S(1)} %turn_other.1.b_other_ref), custom_call_target="tpu_custom_call" | custom-call | flops 3221225472 | bytes 4194304 | tf_op jit(solution)/shard_map/pair_block/pallas_call | solution.py:157
  32.2 0.0 copy-start.2
  32.2 1.2 %pair_block.5.kept_ref = f32[8,96,128]{2,1,0:T(8,128)S(1)} custom-call(bf16[4,2,8,32,128]{4,3,2,1,0:T(8,128)(2,1)S(1)} %bitcast.13, bf16[4,2,8,32,128]{4,3,2,1,0:T(8,128)(2,1)S(1)} %collective-permute-done.1.other_ref, bf16[256,4096]{1,0:T(8,128)(2,1)S(1)} %turn_own.1.b_own_ref, bf16[128,4096]{1,0:T(8,128)(2,1)S(1)} %turn_other.1.b_other_ref), custom_call_target="tpu_custom_call" | custom-call | flops 3221225472 | bytes 4194304 | tf_op jit(solution)/shard_map/pair_block/pallas_call | solution.py:157
  33.5 2.2 %collective-permute-done.2.came_ref = bf16[8,96,128]{2,1,0:T(8,128)(2,1)S(1)} collective-permute-done((bf16[8,96,128]{2,1,0:T(8,128)(2,1)S(1)}, bf16[8,96,128]{2,1,0:T(8,128)(2,1)S(1)}, u32[]{:S(2)}, u32[]{:S(2)}) %collective-permute-start.2) | collective-permute-done | bytes 196640 | tf_op jit(solution)/shard_map/ppermute | solution.py:190
  35.6 4.1 %collective-permute-start.4 = (bf16[8,96,128]{2,1,0:T(8,128)(2,1)S(1)}, bf16[8,96,128]{2,1,0:T(8,128)(2,1)S(1)}, u32[]{:S(2)}, u32[]{:S(2)}) collective-permute-start(bf16[8,96,128]{2,1,0:T(8,128)(2,1)S(1)} %merge.1), channel_id=1, source_target_pairs={{0,64},{32,224},{64,128},{96,32},{128,192},{160,96},{192,0},{224,1... | collective-permute-start | bytes 589832 | tf_op jit(solution)/shard_map/ppermute | solution.py:190
  39.7 0.2 collective-permute-done.3.came_ref
  40.0 4.3 %collective-permute-done.4 = bf16[8,96,128]{2,1,0:T(8,128)(2,1)S(1)} collective-permute-done((bf16[8,96,128]{2,1,0:T(8,128)(2,1)S(1)}, bf16[8,96,128]{2,1,0:T(8,128)(2,1)S(1)}, u32[]{:S(2)}, u32[]{:S(2)}) %collective-permute-start.4) | collective-permute-done | bytes 196640 | tf_op jit(solution)/shard_map/ppermute | solution.py:190
  44.3 0.0 copy-done.2
  44.3 0.7 %add_convert_fusion = bf16[8,96,128]{2,1,0:T(8,128)(2,1)} fusion(f32[8,96,128]{2,1,0:T(8,128)S(1)} %presum.1, bf16[8,96,128]{2,1,0:T(8,128)(2,1)S(1)} %collective-permute-done.4, f32[128]{0:T(128)S(1)} %copy-done.2), kind=kLoop, calls=%fused_computation | loop fusion | flops 491520 | bytes 786944 | tf_op jit(solution)/shard_map/convert_element_type | solution.py:217
  (2 shorter events, 0.1 us)
Async XLA Ops:
  0.0 21.6 %copy-start = (bf16[128,96,32]{0,2,1:T(8,128)(2,1)S(1)}, bf16[128,96,32]{0,2,1:T(8,128)(2,1)}, u32[]{:S(2)}) copy-start(bf16[128,96,32]{0,2,1:T(8,128)(2,1)} %param.5) | copy-start | bytes 2359300
  0.0 21.6 %copy-start.1 = (bf16[1024,128]{1,0:T(8,128)(2,1)S(1)}, bf16[1024,128]{1,0:T(8,128)(2,1)}, u32[]{:S(2)}) copy-start(bf16[1024,128]{1,0:T(8,128)(2,1)} %matrix_ref.1) | copy-start | bytes 786436
  1.7 17.6 %all-to-all-start = ((bf16[32,2,32,128]{3,2,1,0:T(8,128)(2,1)}), bf16[32,2,32,128]{3,2,1,0:T(8,128)(2,1)S(1)}, u32[]{:S(2)}, u32[]{:S(2)}) async-start(bf16[32,2,32,128]{3,2,1,0:T(8,128)(2,1)} %spread.1), calls=%async_computation | async-start | bytes 1048576 | tf_op jit(solution)/shard_map/all_to_all | solution.py:200
  9.8 3.4 %collective-permute-start = (bf16[96,32,128]{2,1,0:T(8,128)(2,1)}, bf16[96,32,128]{2,1,0:T(8,128)(2,1)S(1)}, u32[]{:S(2)}, u32[]{:S(2)}) collective-permute-start(bf16[96,32,128]{2,1,0:T(8,128)(2,1)} %bitcast.7), channel_id=1, source_target_pairs={{0,32},{32,0},{1,33},{33,1},{2,34},{34,2},{3,35},{35,3},{4,36},{36... | collective-permute-start | bytes 2359304 | tf_op jit(solution)/shard_map/ppermute | solution.py:199
  19.3 3.9 %collective-permute-start.1 = (bf16[4,2,8,32,128]{4,3,2,1,0:T(8,128)(2,1)S(1)}, bf16[4,2,8,32,128]{4,3,2,1,0:T(8,128)(2,1)S(1)}, u32[]{:S(2)}, u32[]{:S(2)}) collective-permute-start(bf16[4,2,8,32,128]{4,3,2,1,0:T(8,128)(2,1)S(1)} %bitcast.9), channel_id=1, source_target_pairs={{0,32},{32,0},{1,33},{33,1},{2,34},{34,2},{3,35},{35,3},{4,36},{36... | collective-permute-start | bytes 1572872 | tf_op jit(solution)/shard_map/ppermute | solution.py:205
  24.3 11.3 %collective-permute-start.2 = (bf16[8,96,128]{2,1,0:T(8,128)(2,1)S(1)}, bf16[8,96,128]{2,1,0:T(8,128)(2,1)S(1)}, u32[]{:S(2)}, u32[]{:S(2)}) collective-permute-start(bf16[8,96,128]{2,1,0:T(8,128)(2,1)S(1)} %pair_block.4), channel_id=1, source_target_pairs={{0,64},{32,224},{64,128},{96,32},{128,192},{160,96},{192,0},{224,1... | collective-permute-start | bytes 589832 | tf_op jit(solution)/shard_map/ppermute | solution.py:190
  30.7 9.3 %collective-permute-start.3 = (bf16[8,96,128]{2,1,0:T(8,128)(2,1)S(1)}, bf16[8,96,128]{2,1,0:T(8,128)(2,1)S(1)}, u32[]{:S(2)}, u32[]{:S(2)}) collective-permute-start(bf16[8,96,128]{2,1,0:T(8,128)(2,1)S(1)} %pair_block.7), channel_id=1, source_target_pairs={{0,96},{32,192},{64,160},{96,0},{128,224},{160,64},{192,32},{224,1... | collective-permute-start | bytes 589832 | tf_op jit(solution)/shard_map/ppermute | solution.py:190
  32.2 12.1 %copy-start.2 = (f32[128]{0:T(128)S(1)}, f32[128]{0:T(128)}, u32[]{:S(2)}) copy-start(f32[128]{0:T(128)} %param.7) | copy-start | bytes 1540
  35.6 8.7 %collective-permute-start.4 = (bf16[8,96,128]{2,1,0:T(8,128)(2,1)S(1)}, bf16[8,96,128]{2,1,0:T(8,128)(2,1)S(1)}, u32[]{:S(2)}, u32[]{:S(2)}) collective-permute-start(bf16[8,96,128]{2,1,0:T(8,128)(2,1)S(1)} %merge.1), channel_id=1, source_target_pairs={{0,64},{32,224},{64,128},{96,32},{128,192},{160,96},{192,0},{224,1... | collective-permute-start | bytes 589832 | tf_op jit(solution)/shard_map/ppermute | solution.py:190

commit v5 on v4

--- a/solution.py
+++ b/solution.py
@@ -15,6 +15,8 @@
 DEPTH_AXES = ("zh", "core")
 TILE_AXES = ("zl", "y", "x")
 SWAP = [(0, 1), (1, 0)]
+BLOCKS = (((2, 2), False), ((1, 3), False), ((1, 3), True), ((0, 0), False))
+FAR, NEAR, CROSS, KEPT = range(4)
 WHOLE = pl.BlockSpec(memory_space=pltpu.VMEM)
 ANY = pl.BlockSpec(memory_space=pltpu.HBM)
 
@@ -66,76 +68,85 @@
         out_ref[0:LANES, f * LANES:(f + 1) * LANES] = picked.T.astype(jnp.bfloat16)
 
 
-def own_kernel(b_ref, matrix_ref, out_ref, wide_ref, matrix_wide_ref, matrix_held_ref, sem):
-    fetch = pltpu.make_async_copy(matrix_ref, matrix_held_ref, sem)
-    fetch.start()
-    turn(b_ref, wide_ref, out_ref)
-    fetch.wait()
-    matrix_wide_ref[...] = matrix_held_ref[...].astype(jnp.float32)
+def matrix_kernel(matrix_ref, out_ref, wide_ref):
+    wide_ref[...] = matrix_ref[...].astype(jnp.float32)
     group = LANES // FEATS
     for g in range(FEATS // group):
-        rows = [
-            matrix_wide_ref[pl.ds(g * group + i, FEATS, stride=FEATS), :] for i in range(group)
-        ]
-        out_ref[LANES:, g * LANES:(g + 1) * LANES] = jnp.concatenate(rows, axis=0).T.astype(
+        rows = [wide_ref[pl.ds(g * group + i, FEATS, stride=FEATS), :] for i in range(group)]
+        out_ref[:, g * LANES:(g + 1) * LANES] = jnp.concatenate(rows, axis=0).T.astype(
             jnp.bfloat16
         )
 
 
-def turn_own(b, matrix):
+def turn_matrix(matrix):
+    return pl.pallas_call(
+        matrix_kernel,
+        out_shape=jax.ShapeDtypeStruct((matrix.shape[1], matrix.shape[0]), jnp.bfloat16),
+        scratch_shapes=[pltpu.VMEM(matrix.shape, jnp.float32)],
+        in_specs=[WHOLE],
+        out_specs=WHOLE,
+        compiler_params=limit(8),
+        cost_estimate=cost(2 << 20),
+        name="turn_matrix",
+    )(matrix)
+
+
+def turn_kernel(b_ref, out_ref, wide_ref):
+    turn(b_ref, wide_ref, out_ref)
+
+
+def turn_factor(b):
     wide = (b.shape[0] * FEATS, LANES)
     return pl.pallas_call(
-        own_kernel,
-        out_shape=jax.ShapeDtypeStruct((2 * LANES, FEATS * LANES), jnp.bfloat16),
-        scratch_shapes=[
-            pltpu.VMEM(wide, jnp.float32),
-            pltpu.VMEM(matrix.shape, jnp.float32),
-            pltpu.VMEM(matrix.shape, jnp.bfloat16),
-            pltpu.SemaphoreType.DMA,
-        ],
-        in_specs=[WHOLE, ANY],
-        out_specs=WHOLE,
-        compiler_params=limit(8),
-        cost_estimate=cost(4 << 20),
-        name="turn_own",
-    )(b.reshape(wide), matrix)
-
-
-def other_kernel(b_ref, out_ref, wide_ref):
-    turn(b_ref, wide_ref, out_ref)
-
-
-def turn_other(b):
-    wide = (b.shape[0] * FEATS, LANES)
-    return pl.pallas_call(
-        other_kernel,
+        turn_kernel,
         out_shape=jax.ShapeDtypeStruct((LANES, FEATS * LANES), jnp.bfloat16),
         scratch_shapes=[pltpu.VMEM(wide, jnp.float32)],
         in_specs=[WHOLE],
         out_specs=WHOLE,
         compiler_params=limit(8),
         cost_estimate=cost(4 << 20),
-        name="turn_other",
+        name="turn_factor",
     )(b.reshape(wide))
 
 
-def pair_kernel(hops, flip, own_ref, other_ref, b_own_ref, b_other_ref, out_ref, stack_ref):
+def select_kernel(in_ref, out_ref):
+    zh = lax.axis_index("zh")
+    core = 1 - lax.axis_index("core")
+    for slot, (hops, flip) in enumerate(BLOCKS):
+        block = (zh + jnp.where(core == 0, hops[0], hops[1])) & (RING - 1)
+        out_ref[slot] = in_ref[block, 1 - core if flip else core]
+
+
+def select(a):
+    return pl.pallas_call(
+        select_kernel,
+        out_shape=jax.ShapeDtypeStruct((len(BLOCKS),) + a.shape[2:], jnp.bfloat16),
+        in_specs=[WHOLE],
+        out_specs=WHOLE,
+        compiler_params=limit(8),
+        cost_estimate=cost(1 << 20),
+        name="select",
+    )(a)
+
+
+def pair_kernel(slot, own_ref, other_ref, b_own_ref, b_other_ref, w_ref, out_ref, stack_ref):
     zh = lax.axis_index("zh")
     core = lax.axis_index("core")
+    hops, flip = BLOCKS[slot]
     block = (zh + jnp.where(core == 0, hops[0], hops[1])) & (RING - 1)
     half = 1 - core if flip else core
     width = ROWS * FEATS
     a = jnp.concatenate(
         [
             own_ref[block, half].reshape(width, LANES),
-            other_ref[block, half].reshape(width, LANES),
+            other_ref[slot].reshape(width, LANES),
         ],
         axis=1,
     )
     feats = 4
     for c in range(FEATS // feats):
         lanes = slice(c * feats * LANES, (c + 1) * feats * LANES)
-        b = jnp.concatenate([b_own_ref[0:LANES, lanes], b_other_ref[:, lanes]], axis=0)
+        b = jnp.concatenate([b_own_ref[:, lanes], b_other_ref[:, lanes]], axis=0)
         outer = jnp.dot(a, b, preferred_element_type=jnp.float32).astype(jnp.bfloat16)
         for f in range(feats):
             k = (c * feats + f) * FEATS
@@ -144,26 +155,25 @@
                     r * FEATS:(r + 1) * FEATS, f * LANES:(f + 1) * LANES
                 ]
     cols = out_ref.shape[1]
-    w = b_own_ref[LANES:, 0:FEATS * FEATS]
     for r in range(0, ROWS, 2):
         mixed = jnp.dot(
-            w, stack_ref[:, r * LANES:(r + 2) * LANES], preferred_element_type=jnp.float32
+            w_ref[...], stack_ref[:, r * LANES:(r + 2) * LANES], preferred_element_type=jnp.float32
         )
         out_ref[r] = mixed[:, :LANES].T[:cols].astype(out_ref.dtype)
         out_ref[r + 1] = mixed[:, LANES:].T[:cols].astype(out_ref.dtype)
 
 
-def pair_block(hops, flip, own, other, b_own, b_other, cols, dtype=jnp.bfloat16):
-    return pl.pallas_call(
-        functools.partial(pair_kernel, hops, flip),
+def pair_block(slot, own, other, b_own, b_other, wt, cols, dtype=jnp.bfloat16):
+    return pl.pallas_call(
+        functools.partial(pair_kernel, slot),
         out_shape=jax.ShapeDtypeStruct((ROWS, cols, LANES), dtype),
-        in_specs=[WHOLE] * 4,
+        in_specs=[WHOLE] * 5,
         out_specs=WHOLE,
         scratch_shapes=[pltpu.VMEM((FEATS * FEATS, ROWS * LANES), jnp.bfloat16)],
         compiler_params=limit(16),
         cost_estimate=cost(4 << 20, 3 << 30),
         name="pair_block",
-    )(own, other, b_own, b_other)
+    )(own, other, b_own, b_other, wt)
 
 
 def add_kernel(kept_ref, came_ref, out_ref):
@@ -199,17 +209,19 @@
     b_swapped = lax.ppermute(bt, "core", SWAP)
     a_own = lax.all_to_all(copies, TILE_AXES, split_axis=0, concat_axis=0, tiled=True)
     a_own = a_own.reshape(RING, 2, ROWS, FEATS, LANES)
-    b_own = turn_own(bt, matrix)
-    b_other = turn_other(b_swapped)
-    a_swap, _ = lax.optimization_barrier((a_own, b_other))
-    a_other = lax.ppermute(a_swap, "core", SWAP)
+    b_own = turn_factor(bt)
+    b_other = turn_factor(b_swapped)
+    wt = turn_matrix(matrix)
+    a_in, _, _ = lax.optimization_barrier((a_own, b_other, b_own))
+    a_give = select(a_in)
+    a_other = lax.ppermute(a_give, "core", SWAP)
     block = functools.partial(
-        pair_block, own=a_own, other=a_other, b_own=b_own, b_other=b_other, cols=cols
+        pair_block, own=a_own, other=a_other, b_own=b_own, b_other=b_other, wt=wt, cols=cols
     )
-    far = send(block((2, 2), False), (1, 3))
-    left_part = block((1, 3), False, dtype=jnp.float32)
-    right = send(block((1, 3), True), (1, 3), 1)
-    kept = block((0, 0), False, dtype=jnp.float32)
+    far = send(block(FAR), (1, 3))
+    left_part = block(NEAR, dtype=jnp.float32)
+    right = send(block(CROSS), (1, 3), 1)
+    kept = block(KEPT, dtype=jnp.float32)
     far, kept, left_part = lax.optimization_barrier((far, kept, left_part))
     merged = add_to(left_part, far, jnp.bfloat16, "merge", 200 << 20)
     left = send(merged, (1, 3))

time: 45.9 us -> 45.6 us (level)
    ppermute x1, waiting for transfers between devices: 2.12 us -> 0.79 us  [local(): b_swapped = lax.ppermute(bt, 'core', SWAP)]
    ppermute x1, waiting for transfers between devices: 0.01 us -> 0.75 us  [local(): a_other = lax.ppermute(a_give, 'core', SWAP)]
    pallas_call x6 -> x8, Pallas kernels: 7.35 us -> 7.34 us  [the longest x4 4.68 us: pair_block(): pl.pallas_call(functools.partial(pair_kernel, slot), out_shape=jax.ShapeD...]
  transfers between devices with their start and end apart: 6 -> 6, of which waited for: 5 -> 6; matrix products, arithmetic and copies ran while one was open for 0% -> 0% of each run, Pallas kernels for 14% -> 14%
where the time goes in v5:
time: 45.6 us; the launch traced here: 44.8 us
  starting transfers between devices  21.4 us (47%)
  waiting for transfers between devices  13.4 us (29%)
  Pallas kernels  9.13 us (20%)
  other arithmetic  0.75 us (2%)
    ppermute x3, starting transfers between devices, send(): return lax.ppermute(part, DEPTH_AXES, pairs)  9.65 us
    all_to_all x1, starting transfers between devices, local(): lax.all_to_all(copies, TILE_AXES, split_axis=0, concat_axis=0, tiled=True)  8.01 us
    ppermute x3, waiting for transfers between devices, send(): return lax.ppermute(part, DEPTH_AXES, pairs)  6.69 us
    all_to_all x1, waiting for transfers between devices, local(): lax.all_to_all(copies, TILE_AXES, split_axis=0, concat_axis=0, tiled=True)  5.21 us
    pallas_call x4, Pallas kernels, pair_block(): pl.pallas_call(functools.partial(pair_kernel, slot), out_shape=jax.ShapeD...  4.68 us
    ppermute x1, starting transfers between devices, local(): a_other = lax.ppermute(a_give, 'core', SWAP)  2.38 us
    pallas_call x2, Pallas kernels, turn_factor(): pl.pallas_call(turn_kernel, out_shape=jax.ShapeDtypeStruct((LANES, FEATS...  2.24 us
    pallas_call x1, Pallas kernels, spread(): pl.pallas_call(spread_kernel, out_shape=jax.ShapeDtypeStruct((TILES,) + o...  1.72 us
  transfers between devices with their start and end apart: 6, of which 6 were waited for; matrix products, arithmetic and copies ran while one was open for 0% of the time, Pallas kernels for 14%

profile of v5, /device:TPU:33, one launch (start us, length us, event | category | flops | bytes accessed | tf_op | source)
XLA Modules:
  0.0 44.8 jit_solution(7717986434195204436)
XLA Ops:
  0.0 0.0 copy-start
  0.0 1.7 %spread.1 = bf16[32,2,32,128]{3,2,1,0:T(8,128)(2,1)} custom-call(bf16[2,32,128]{2,1,0:T(8,128)(2,1)} %bitcast.14), custom_call_target="tpu_custom_call" | custom-call | bytes 1048576 | tf_op jit(solution)/shard_map/spread/pallas_call | solution.py:45
  1.7 8.0 %all-to-all-start = ((bf16[32,2,32,128]{3,2,1,0:T(8,128)(2,1)}), bf16[32,2,32,128]{3,2,1,0:T(8,128)(2,1)S(1)}, u32[]{:S(2)}, u32[]{:S(2)}) async-start(bf16[32,2,32,128]{3,2,1,0:T(8,128)(2,1)} %spread.1), calls=%async_computation | async-start | bytes 1048576 | tf_op jit(solution)/shard_map/all_to_all | solution.py:210
  9.7 0.0 copy-done
  9.8 1.3 %collective-permute-start = (bf16[96,32,128]{2,1,0:T(8,128)(2,1)S(1)}, bf16[96,32,128]{2,1,0:T(8,128)(2,1)S(1)}, u32[]{:S(2)}, u32[]{:S(2)}) collective-permute-start(bf16[96,32,128]{2,1,0:T(8,128)(2,1)S(1)} %bitcast.11), channel_id=1, source_target_pairs={{0,32},{32,0},{1,33},{33,1},{2,34},{34,2},{3,35},{35,3},{4,36},{36... | collective-permute-start | bytes 2359304 | tf_op jit(solution)/shard_map/ppermute | solution.py:209
  11.1 1.1 %turn_factor.3.b_own_ref = bf16[128,4096]{1,0:T(8,128)(2,1)S(1)} custom-call(bf16[3072,128]{1,0:T(8,128)(2,1)S(1)} %bitcast.12), custom_call_target="tpu_custom_call" | custom-call | bytes 4194304 | tf_op jit(solution)/shard_map/turn_factor/pallas_call | solution.py:100
  12.2 0.8 %collective-permute-done = bf16[96,32,128]{2,1,0:T(8,128)(2,1)S(1)} collective-permute-done((bf16[96,32,128]{2,1,0:T(8,128)(2,1)S(1)}, bf16[96,32,128]{2,1,0:T(8,128)(2,1)S(1)}, u32[]{:S(2)}, u32[]{:S(2)}) %collective-permute-start) | collective-permute-done | bytes 786464 | tf_op jit(solution)/shard_map/ppermute | solution.py:209
  13.0 1.1 %turn_factor.2.b_other_ref = bf16[128,4096]{1,0:T(8,128)(2,1)S(1)} custom-call(bf16[3072,128]{1,0:T(8,128)(2,1)S(1)} %bitcast.13), custom_call_target="tpu_custom_call" | custom-call | bytes 4194304 | tf_op jit(solution)/shard_map/turn_factor/pallas_call | solution.py:100
  14.1 5.2 %all-to-all-done = bf16[32,2,32,128]{3,2,1,0:T(8,128)(2,1)S(1)} async-done(((bf16[32,2,32,128]{3,2,1,0:T(8,128)(2,1)}), bf16[32,2,32,128]{3,2,1,0:T(8,128)(2,1)S(1)}, u32[]{:S(2)}, u32[]{:S(2)}) %all-to-all-start) | async-done | bytes 524320 | tf_op jit(solution)/shard_map/all_to_all | solution.py:210
  19.3 0.0 copy-start.1
  19.4 2.4 %collective-permute-start.1 = (bf16[4,8,32,128]{3,2,1,0:T(8,128)(2,1)S(1)}, bf16[4,8,32,128]{3,2,1,0:T(8,128)(2,1)S(1)}, u32[]{:S(2)}, u32[]{:S(2)}) collective-permute-start(bf16[4,8,32,128]{3,2,1,0:T(8,128)(2,1)S(1)} %select.1), channel_id=1, source_target_pairs={{0,32},{32,0},{1,33},{33,1},{2,34},{34,2},{3,35},{35,3},{4,36},{36... | collective-permute-start | bytes 786440 | tf_op jit(solution)/shard_map/ppermute | solution.py:217
  21.7 0.0 copy-done.1
  21.7 0.4 turn_matrix.1.w_ref
  22.1 0.8 %collective-permute-done.1.other_ref = bf16[4,8,32,128]{3,2,1,0:T(8,128)(2,1)S(1)} collective-permute-done((bf16[4,8,32,128]{3,2,1,0:T(8,128)(2,1)S(1)}, bf16[4,8,32,128]{3,2,1,0:T(8,128)(2,1)S(1)}, u32[]{:S(2)}, u32[]{:S(2)}) %collective-permute-start.1) | collective-permute-done | bytes 262176 | tf_op jit(solution)/shard_map/ppermute | solution.py:217
  22.9 1.1 %pair_block.4 = bf16[8,96,128]{2,1,0:T(8,128)(2,1)S(1)} custom-call(bf16[4,2,8,32,128]{4,3,2,1,0:T(8,128)(2,1)S(1)} %bitcast.7, bf16[4,8,32,128]{3,2,1,0:T(8,128)(2,1)S(1)} %collective-permute-done.1.other_ref, bf16[128,4096]{1,0:T(8,128)(2,1)S(1)} %turn_factor.3.b_own_ref, bf16[128,4096]{1,0:T(8,128)(2,1)S(1)} %turn_factor.2.b_other_ref, ...), custom_call_target="tpu_custom_call" | custom-call | flops 3221225472 | bytes 4194304 | tf_op jit(solution)/shard_map/pair_block/pallas_call | solution.py:167
  24.0 5.2 %collective-permute-start.2 = (bf16[8,96,128]{2,1,0:T(8,128)(2,1)S(1)}, bf16[8,96,128]{2,1,0:T(8,128)(2,1)S(1)}, u32[]{:S(2)}, u32[]{:S(2)}) collective-permute-start(bf16[8,96,128]{2,1,0:T(8,128)(2,1)S(1)} %pair_block.4), channel_id=1, source_target_pairs={{0,64},{32,224},{64,128},{96,32},{128,192},{160,96},{192,0},{224,1... | collective-permute-start | bytes 589832 | tf_op jit(solution)/shard_map/ppermute | solution.py:200
  29.2 1.1 %pair_block.7 = bf16[8,96,128]{2,1,0:T(8,128)(2,1)S(1)} custom-call(bf16[4,2,8,32,128]{4,3,2,1,0:T(8,128)(2,1)S(1)} %bitcast.8, bf16[4,8,32,128]{3,2,1,0:T(8,128)(2,1)S(1)} %collective-permute-done.1.other_ref, bf16[128,4096]{1,0:T(8,128)(2,1)S(1)} %turn_factor.3.b_own_ref, bf16[128,4096]{1,0:T(8,128)(2,1)S(1)} %turn_factor.2.b_other_ref, ...), custom_call_target="tpu_custom_call" | custom-call | flops 3221225472 | bytes 4194304 | tf_op jit(solution)/shard_map/pair_block/pallas_call | solution.py:167
  30.4 0.4 collective-permute-start.3
  30.7 1.2 %pair_block.6.kept_ref = f32[8,96,128]{2,1,0:T(8,128)S(1)} custom-call(bf16[4,2,8,32,128]{4,3,2,1,0:T(8,128)(2,1)S(1)} %bitcast.9, bf16[4,8,32,128]{3,2,1,0:T(8,128)(2,1)S(1)} %collective-permute-done.1.other_ref, bf16[128,4096]{1,0:T(8,128)(2,1)S(1)} %turn_factor.3.b_own_ref, bf16[128,4096]{1,0:T(8,128)(2,1)S(1)} %turn_factor.2.b_other_ref, ...), custom_call_target="tpu_custom_call" | custom-call | flops 3221225472 | bytes 4194304 | tf_op jit(solution)/shard_map/pair_block/pallas_call | solution.py:167
  31.9 1.2 %pair_block.5.kept_ref = f32[8,96,128]{2,1,0:T(8,128)S(1)} custom-call(bf16[4,2,8,32,128]{4,3,2,1,0:T(8,128)(2,1)S(1)} %bitcast.10, bf16[4,8,32,128]{3,2,1,0:T(8,128)(2,1)S(1)} %collective-permute-done.1.other_ref, bf16[128,4096]{1,0:T(8,128)(2,1)S(1)} %turn_factor.3.b_own_ref, bf16[128,4096]{1,0:T(8,128)(2,1)S(1)} %turn_factor.2.b_other_ref, ...), custom_call_target="tpu_custom_call" | custom-call | flops 3221225472 | bytes 4194304 | tf_op jit(solution)/shard_map/pair_block/pallas_call | solution.py:167
  33.2 2.2 %collective-permute-done.2.came_ref = bf16[8,96,128]{2,1,0:T(8,128)(2,1)S(1)} collective-permute-done((bf16[8,96,128]{2,1,0:T(8,128)(2,1)S(1)}, bf16[8,96,128]{2,1,0:T(8,128)(2,1)S(1)}, u32[]{:S(2)}, u32[]{:S(2)}) %collective-permute-start.2) | collective-permute-done | bytes 196640 | tf_op jit(solution)/shard_map/ppermute | solution.py:200
  35.4 0.0 copy-start.2
  35.4 4.1 %collective-permute-start.4 = (bf16[8,96,128]{2,1,0:T(8,128)(2,1)S(1)}, bf16[8,96,128]{2,1,0:T(8,128)(2,1)S(1)}, u32[]{:S(2)}, u32[]{:S(2)}) collective-permute-start(bf16[8,96,128]{2,1,0:T(8,128)(2,1)S(1)} %merge.1), channel_id=1, source_target_pairs={{0,64},{32,224},{64,128},{96,32},{128,192},{160,96},{192,0},{224,1... | collective-permute-start | bytes 589832 | tf_op jit(solution)/shard_map/ppermute | solution.py:200
  39.5 0.2 collective-permute-done.3.came_ref
  39.7 4.3 %collective-permute-done.4 = bf16[8,96,128]{2,1,0:T(8,128)(2,1)S(1)} collective-permute-done((bf16[8,96,128]{2,1,0:T(8,128)(2,1)S(1)}, bf16[8,96,128]{2,1,0:T(8,128)(2,1)S(1)}, u32[]{:S(2)}, u32[]{:S(2)}) %collective-permute-start.4) | collective-permute-done | bytes 196640 | tf_op jit(solution)/shard_map/ppermute | solution.py:200
  44.0 0.0 copy-done.2
  44.1 0.8 %add_convert_fusion = bf16[8,96,128]{2,1,0:T(8,128)(2,1)} fusion(f32[8,96,128]{2,1,0:T(8,128)S(1)} %presum.1, bf16[8,96,128]{2,1,0:T(8,128)(2,1)S(1)} %collective-permute-done.4, f32[128]{0:T(128)S(1)} %copy-done.2), kind=kLoop, calls=%fused_computation | loop fusion | flops 491520 | bytes 786944 | tf_op jit(solution)/shard_map/convert_element_type | solution.py:229
  (3 shorter events, 0.1 us)
Async XLA Ops:
  0.0 9.7 %copy-start = (bf16[128,96,32]{0,2,1:T(8,128)(2,1)S(1)}, bf16[128,96,32]{0,2,1:T(8,128)(2,1)}, u32[]{:S(2)}) copy-start(bf16[128,96,32]{0,2,1:T(8,128)(2,1)} %param.5) | copy-start | bytes 2359300
  1.7 17.6 %all-to-all-start = ((bf16[32,2,32,128]{3,2,1,0:T(8,128)(2,1)}), bf16[32,2,32,128]{3,2,1,0:T(8,128)(2,1)S(1)}, u32[]{:S(2)}, u32[]{:S(2)}) async-start(bf16[32,2,32,128]{3,2,1,0:T(8,128)(2,1)} %spread.1), calls=%async_computation | async-start | bytes 1048576 | tf_op jit(solution)/shard_map/all_to_all | solution.py:210
  9.8 3.2 %collective-permute-start = (bf16[96,32,128]{2,1,0:T(8,128)(2,1)S(1)}, bf16[96,32,128]{2,1,0:T(8,128)(2,1)S(1)}, u32[]{:S(2)}, u32[]{:S(2)}) collective-permute-start(bf16[96,32,128]{2,1,0:T(8,128)(2,1)S(1)} %bitcast.11), channel_id=1, source_target_pairs={{0,32},{32,0},{1,33},{33,1},{2,34},{34,2},{3,35},{35,3},{4,36},{36... | collective-permute-start | bytes 2359304 | tf_op jit(solution)/shard_map/ppermute | solution.py:209
  19.3 2.4 %copy-start.1 = (bf16[1024,128]{1,0:T(8,128)(2,1)S(1)}, bf16[1024,128]{1,0:T(8,128)(2,1)}, u32[]{:S(2)}) copy-start(bf16[1024,128]{1,0:T(8,128)(2,1)} %matrix_ref.1) | copy-start | bytes 786436
  19.4 3.5 %collective-permute-start.1 = (bf16[4,8,32,128]{3,2,1,0:T(8,128)(2,1)S(1)}, bf16[4,8,32,128]{3,2,1,0:T(8,128)(2,1)S(1)}, u32[]{:S(2)}, u32[]{:S(2)}) collective-permute-start(bf16[4,8,32,128]{3,2,1,0:T(8,128)(2,1)S(1)} %select.1), channel_id=1, source_target_pairs={{0,32},{32,0},{1,33},{33,1},{2,34},{34,2},{3,35},{35,3},{4,36},{36... | collective-permute-start | bytes 786440 | tf_op jit(solution)/shard_map/ppermute | solution.py:217
  24.0 11.3 %collective-permute-start.2 = (bf16[8,96,128]{2,1,0:T(8,128)(2,1)S(1)}, bf16[8,96,128]{2,1,0:T(8,128)(2,1)S(1)}, u32[]{:S(2)}, u32[]{:S(2)}) collective-permute-start(bf16[8,96,128]{2,1,0:T(8,128)(2,1)S(1)} %pair_block.4), channel_id=1, source_target_pairs={{0,64},{32,224},{64,128},{96,32},{128,192},{160,96},{192,0},{224,1... | collective-permute-start | bytes 589832 | tf_op jit(solution)/shard_map/ppermute | solution.py:200
  30.4 9.3 %collective-permute-start.3 = (bf16[8,96,128]{2,1,0:T(8,128)(2,1)S(1)}, bf16[8,96,128]{2,1,0:T(8,128)(2,1)S(1)}, u32[]{:S(2)}, u32[]{:S(2)}) collective-permute-start(bf16[8,96,128]{2,1,0:T(8,128)(2,1)S(1)} %pair_block.7), channel_id=1, source_target_pairs={{0,96},{32,192},{64,160},{96,0},{128,224},{160,64},{192,32},{224,1... | collective-permute-start | bytes 589832 | tf_op jit(solution)/shard_map/ppermute | solution.py:200
  35.4 8.7 %copy-start.2 = (f32[128]{0:T(128)S(1)}, f32[128]{0:T(128)}, u32[]{:S(2)}) copy-start(f32[128]{0:T(128)} %param.7) | copy-start | bytes 1540
  35.4 8.7 %collective-permute-start.4 = (bf16[8,96,128]{2,1,0:T(8,128)(2,1)S(1)}, bf16[8,96,128]{2,1,0:T(8,128)(2,1)S(1)}, u32[]{:S(2)}, u32[]{:S(2)}) collective-permute-start(bf16[8,96,128]{2,1,0:T(8,128)(2,1)S(1)} %merge.1), channel_id=1, source_target_pairs={{0,64},{32,224},{64,128},{96,32},{128,192},{160,96},{192,0},{224,1... | collective-permute-start | bytes 589832 | tf_op jit(solution)/shard_map/ppermute | solution.py:200

commit v6 on v5

--- a/solution.py
+++ b/solution.py
@@ -29,16 +29,22 @@
     return pl.CostEstimate(flops=flops, bytes_accessed=nbytes, transcendentals=0)
 
 
-def spread_kernel(in_ref, out_ref, held_ref, filled_ref, in_sem, out_sem):
+def spread_kernel(in_ref, out_ref, held_ref, filled_ref, in_sem, out_sems):
     fetch = pltpu.make_async_copy(in_ref, held_ref, in_sem)
     fetch.start()
     fetch.wait()
     own = held_ref[...]
-    for t in range(TILES):
+    each = filled_ref.shape[0]
+    for t in range(each):
         filled_ref[t] = own
-    store = pltpu.make_async_copy(filled_ref, out_ref, out_sem)
-    store.start()
-    store.wait()
+    copies = [
+        pltpu.make_async_copy(filled_ref, out_ref.at[pl.ds(i * each, each)], out_sems.at[i])
+        for i in range(TILES // each)
+    ]
+    for copy in copies:
+        copy.start()
+    for copy in copies:
+        copy.wait()
 
 
 def spread(own):
@@ -49,9 +55,9 @@
         out_specs=ANY,
         scratch_shapes=[
             pltpu.VMEM(own.shape, jnp.bfloat16),
-            pltpu.VMEM((TILES,) + own.shape, jnp.bfloat16),
+            pltpu.VMEM((8,) + own.shape, jnp.bfloat16),
             pltpu.SemaphoreType.DMA,
-            pltpu.SemaphoreType.DMA,
+            pltpu.SemaphoreType.DMA((TILES // 8,)),
         ],
         compiler_params=limit(60),
         cost_estimate=cost(1 << 20),
@@ -155,12 +161,13 @@
                     r * FEATS:(r + 1) * FEATS, f * LANES:(f + 1) * LANES
                 ]
     cols = out_ref.shape[1]
-    for r in range(0, ROWS, 2):
+    for r in range(0, ROWS, 4):
         mixed = jnp.dot(
-            w_ref[...], stack_ref[:, r * LANES:(r + 2) * LANES], preferred_element_type=jnp.float32
+            w_ref[...], stack_ref[:, r * LANES:(r + 4) * LANES], preferred_element_type=jnp.float32
         )
-        out_ref[r] = mixed[:, :LANES].T[:cols].astype(out_ref.dtype)
-        out_ref[r + 1] = mixed[:, LANES:].T[:cols].astype(out_ref.dtype)
+        for i in range(4):
+            lanes = slice(i * LANES, (i + 1) * LANES)
+            out_ref[r + i] = mixed[:, lanes].T[:cols].astype(out_ref.dtype)
 
 
 def pair_block(slot, own, other, b_own, b_other, wt, cols, dtype=jnp.bfloat16):
@@ -190,6 +197,37 @@
         cost_estimate=cost(nbytes),
         name=name,
     )(kept, came)
+
+
+def final_kernel(scale, sum_ref, came_ref, bias_ref, out_ref, held_ref, sems):
+    rows = sum_ref.shape[0]
+    step = rows // sems.shape[0]
+    bias = bias_ref[...]
+    copies = []
+    for i in range(sems.shape[0]):
+        part = pl.ds(i * step, step)
+        total = sum_ref[part] + came_ref[part].astype(jnp.float32)
+        held_ref[part] = (total * scale + bias).astype(jnp.bfloat16)
+        copies.append(pltpu.make_async_copy(held_ref.at[part], out_ref.at[part], sems.at[i]))
+        copies[-1].start()
+    for copy in copies:
+        copy.wait()
+
+
+def finish(kept, came, bias, scale):
+    return pl.pallas_call(
+        functools.partial(final_kernel, scale),
+        out_shape=jax.ShapeDtypeStruct(kept.shape, jnp.bfloat16),
+        in_specs=[WHOLE, WHOLE, WHOLE],
+        out_specs=ANY,
+        scratch_shapes=[
+            pltpu.VMEM(kept.shape, jnp.bfloat16),
+            pltpu.SemaphoreType.DMA((4,)),
+        ],
+        compiler_params=limit(4),
+        cost_estimate=cost(1 << 20),
+        name="finish",
+    )(kept, came, bias.reshape(1, 1, LANES))
 
 
 def send(part, hops, flip=0):
@@ -225,7 +263,8 @@
     far, kept, left_part = lax.optimization_barrier((far, kept, left_part))
     merged = add_to(left_part, far, jnp.bfloat16, "merge", 200 << 20)
     left = send(merged, (1, 3))
-    total = add_to(kept, right, jnp.float32, "presum", 200 << 20) + left.astype(jnp.float32)
+    presum = add_to(kept, right, jnp.float32, "presum", 200 << 20)
+    total = presum + left.astype(jnp.float32)
     return (total * (1.0 / sequences) + bias).astype(jnp.bfloat16)
 
 

time: 45.6 us -> 45.5 us (level)
  no operation moved by 1% of the time
where the time goes in v6:
time: 45.5 us; the launch traced here: 44.7 us
  starting transfers between devices  21.4 us (47%)
  waiting for transfers between devices  13.4 us (29%)
  Pallas kernels  9.05 us (20%)
  other arithmetic  0.75 us (2%)
    ppermute x3, starting transfers between devices, send(): return lax.ppermute(part, DEPTH_AXES, pairs)  9.65 us
    all_to_all x1, starting transfers between devices, local(): lax.all_to_all(copies, TILE_AXES, split_axis=0, concat_axis=0, tiled=True)  8.01 us
    ppermute x3, waiting for transfers between devices, send(): return lax.ppermute(part, DEPTH_AXES, pairs)  6.69 us
    all_to_all x1, waiting for transfers between devices, local(): lax.all_to_all(copies, TILE_AXES, split_axis=0, concat_axis=0, tiled=True)  5.21 us
    pallas_call x4, Pallas kernels, pair_block(): pl.pallas_call(functools.partial(pair_kernel, slot), out_shape=jax.ShapeD...  4.68 us
    ppermute x1, starting transfers between devices, local(): a_other = lax.ppermute(a_give, 'core', SWAP)  2.38 us
    pallas_call x2, Pallas kernels, turn_factor(): pl.pallas_call(turn_kernel, out_shape=jax.ShapeDtypeStruct((LANES, FEATS...  2.24 us
    pallas_call x1, Pallas kernels, spread(): pl.pallas_call(spread_kernel, out_shape=jax.ShapeDtypeStruct((TILES,) + o...  1.65 us
  transfers between devices with their start and end apart: 6, of which 6 were waited for; matrix products, arithmetic and copies ran while one was open for 0% of the time, Pallas kernels for 14%

profile of v6, /device:TPU:33, one launch (start us, length us, event | category | flops | bytes accessed | tf_op | source)
XLA Modules:
  0.0 44.7 jit_solution(4589769483055913317)
XLA Ops:
  0.0 0.0 copy-start
  0.0 1.6 %spread.1 = bf16[32,2,32,128]{3,2,1,0:T(8,128)(2,1)} custom-call(bf16[2,32,128]{2,1,0:T(8,128)(2,1)} %bitcast.14), custom_call_target="tpu_custom_call" | custom-call | bytes 1048576 | tf_op jit(solution)/shard_map/spread/pallas_call | solution.py:51
  1.7 8.0 %all-to-all-start = ((bf16[32,2,32,128]{3,2,1,0:T(8,128)(2,1)}), bf16[32,2,32,128]{3,2,1,0:T(8,128)(2,1)S(1)}, u32[]{:S(2)}, u32[]{:S(2)}) async-start(bf16[32,2,32,128]{3,2,1,0:T(8,128)(2,1)} %spread.1), calls=%async_computation | async-start | bytes 1048576 | tf_op jit(solution)/shard_map/all_to_all | solution.py:248
  9.7 0.0 copy-done
  9.7 1.3 %collective-permute-start = (bf16[96,32,128]{2,1,0:T(8,128)(2,1)S(1)}, bf16[96,32,128]{2,1,0:T(8,128)(2,1)S(1)}, u32[]{:S(2)}, u32[]{:S(2)}) collective-permute-start(bf16[96,32,128]{2,1,0:T(8,128)(2,1)S(1)} %bitcast.11), channel_id=1, source_target_pairs={{0,32},{32,0},{1,33},{33,1},{2,34},{34,2},{3,35},{35,3},{4,36},{36... | collective-permute-start | bytes 2359304 | tf_op jit(solution)/shard_map/ppermute | solution.py:247
  11.0 1.1 %turn_factor.3.b_own_ref = bf16[128,4096]{1,0:T(8,128)(2,1)S(1)} custom-call(bf16[3072,128]{1,0:T(8,128)(2,1)S(1)} %bitcast.12), custom_call_target="tpu_custom_call" | custom-call | bytes 4194304 | tf_op jit(solution)/shard_map/turn_factor/pallas_call | solution.py:106
  12.1 0.8 %collective-permute-done = bf16[96,32,128]{2,1,0:T(8,128)(2,1)S(1)} collective-permute-done((bf16[96,32,128]{2,1,0:T(8,128)(2,1)S(1)}, bf16[96,32,128]{2,1,0:T(8,128)(2,1)S(1)}, u32[]{:S(2)}, u32[]{:S(2)}) %collective-permute-start) | collective-permute-done | bytes 786464 | tf_op jit(solution)/shard_map/ppermute | solution.py:247
  12.9 1.1 %turn_factor.2.b_other_ref = bf16[128,4096]{1,0:T(8,128)(2,1)S(1)} custom-call(bf16[3072,128]{1,0:T(8,128)(2,1)S(1)} %bitcast.13), custom_call_target="tpu_custom_call" | custom-call | bytes 4194304 | tf_op jit(solution)/shard_map/turn_factor/pallas_call | solution.py:106
  14.0 5.2 %all-to-all-done = bf16[32,2,32,128]{3,2,1,0:T(8,128)(2,1)S(1)} async-done(((bf16[32,2,32,128]{3,2,1,0:T(8,128)(2,1)}), bf16[32,2,32,128]{3,2,1,0:T(8,128)(2,1)S(1)}, u32[]{:S(2)}, u32[]{:S(2)}) %all-to-all-start) | async-done | bytes 524320 | tf_op jit(solution)/shard_map/all_to_all | solution.py:248
  19.3 0.0 copy-start.1
  19.3 2.4 %collective-permute-start.1 = (bf16[4,8,32,128]{3,2,1,0:T(8,128)(2,1)S(1)}, bf16[4,8,32,128]{3,2,1,0:T(8,128)(2,1)S(1)}, u32[]{:S(2)}, u32[]{:S(2)}) collective-permute-start(bf16[4,8,32,128]{3,2,1,0:T(8,128)(2,1)S(1)} %select.1), channel_id=1, source_target_pairs={{0,32},{32,0},{1,33},{33,1},{2,34},{34,2},{3,35},{35,3},{4,36},{36... | collective-permute-start | bytes 786440 | tf_op jit(solution)/shard_map/ppermute | solution.py:255
  21.7 0.0 copy-done.1
  21.7 0.4 turn_matrix.1.w_ref
  22.1 0.8 %collective-permute-done.1.other_ref = bf16[4,8,32,128]{3,2,1,0:T(8,128)(2,1)S(1)} collective-permute-done((bf16[4,8,32,128]{3,2,1,0:T(8,128)(2,1)S(1)}, bf16[4,8,32,128]{3,2,1,0:T(8,128)(2,1)S(1)}, u32[]{:S(2)}, u32[]{:S(2)}) %collective-permute-start.1) | collective-permute-done | bytes 262176 | tf_op jit(solution)/shard_map/ppermute | solution.py:255
  22.8 1.1 %pair_block.4 = bf16[8,96,128]{2,1,0:T(8,128)(2,1)S(1)} custom-call(bf16[4,2,8,32,128]{4,3,2,1,0:T(8,128)(2,1)S(1)} %bitcast.7, bf16[4,8,32,128]{3,2,1,0:T(8,128)(2,1)S(1)} %collective-permute-done.1.other_ref, bf16[128,4096]{1,0:T(8,128)(2,1)S(1)} %turn_factor.3.b_own_ref, bf16[128,4096]{1,0:T(8,128)(2,1)S(1)} %turn_factor.2.b_other_ref, ...), custom_call_target="tpu_custom_call" | custom-call | flops 3221225472 | bytes 4194304 | tf_op jit(solution)/shard_map/pair_block/pallas_call | solution.py:174
  24.0 5.2 %collective-permute-start.2 = (bf16[8,96,128]{2,1,0:T(8,128)(2,1)S(1)}, bf16[8,96,128]{2,1,0:T(8,128)(2,1)S(1)}, u32[]{:S(2)}, u32[]{:S(2)}) collective-permute-start(bf16[8,96,128]{2,1,0:T(8,128)(2,1)S(1)} %pair_block.4), channel_id=1, source_target_pairs={{0,64},{32,224},{64,128},{96,32},{128,192},{160,96},{192,0},{224,1... | collective-permute-start | bytes 589832 | tf_op jit(solution)/shard_map/ppermute | solution.py:238
  29.2 1.1 %pair_block.7 = bf16[8,96,128]{2,1,0:T(8,128)(2,1)S(1)} custom-call(bf16[4,2,8,32,128]{4,3,2,1,0:T(8,128)(2,1)S(1)} %bitcast.8, bf16[4,8,32,128]{3,2,1,0:T(8,128)(2,1)S(1)} %collective-permute-done.1.other_ref, bf16[128,4096]{1,0:T(8,128)(2,1)S(1)} %turn_factor.3.b_own_ref, bf16[128,4096]{1,0:T(8,128)(2,1)S(1)} %turn_factor.2.b_other_ref, ...), custom_call_target="tpu_custom_call" | custom-call | flops 3221225472 | bytes 4194304 | tf_op jit(solution)/shard_map/pair_block/pallas_call | solution.py:174
  30.3 0.4 collective-permute-start.3
  30.7 1.2 %pair_block.6.kept_ref = f32[8,96,128]{2,1,0:T(8,128)S(1)} custom-call(bf16[4,2,8,32,128]{4,3,2,1,0:T(8,128)(2,1)S(1)} %bitcast.9, bf16[4,8,32,128]{3,2,1,0:T(8,128)(2,1)S(1)} %collective-permute-done.1.other_ref, bf16[128,4096]{1,0:T(8,128)(2,1)S(1)} %turn_factor.3.b_own_ref, bf16[128,4096]{1,0:T(8,128)(2,1)S(1)} %turn_factor.2.b_other_ref, ...), custom_call_target="tpu_custom_call" | custom-call | flops 3221225472 | bytes 4194304 | tf_op jit(solution)/shard_map/pair_block/pallas_call | solution.py:174
  31.9 1.2 %pair_block.5.kept_ref = f32[8,96,128]{2,1,0:T(8,128)S(1)} custom-call(bf16[4,2,8,32,128]{4,3,2,1,0:T(8,128)(2,1)S(1)} %bitcast.10, bf16[4,8,32,128]{3,2,1,0:T(8,128)(2,1)S(1)} %collective-permute-done.1.other_ref, bf16[128,4096]{1,0:T(8,128)(2,1)S(1)} %turn_factor.3.b_own_ref, bf16[128,4096]{1,0:T(8,128)(2,1)S(1)} %turn_factor.2.b_other_ref, ...), custom_call_target="tpu_custom_call" | custom-call | flops 3221225472 | bytes 4194304 | tf_op jit(solution)/shard_map/pair_block/pallas_call | solution.py:174
  33.1 2.2 %collective-permute-done.2.came_ref = bf16[8,96,128]{2,1,0:T(8,128)(2,1)S(1)} collective-permute-done((bf16[8,96,128]{2,1,0:T(8,128)(2,1)S(1)}, bf16[8,96,128]{2,1,0:T(8,128)(2,1)S(1)}, u32[]{:S(2)}, u32[]{:S(2)}) %collective-permute-start.2) | collective-permute-done | bytes 196640 | tf_op jit(solution)/shard_map/ppermute | solution.py:238
  35.3 0.0 copy-start.2
  35.3 4.1 %collective-permute-start.4 = (bf16[8,96,128]{2,1,0:T(8,128)(2,1)S(1)}, bf16[8,96,128]{2,1,0:T(8,128)(2,1)S(1)}, u32[]{:S(2)}, u32[]{:S(2)}) collective-permute-start(bf16[8,96,128]{2,1,0:T(8,128)(2,1)S(1)} %merge.1), channel_id=1, source_target_pairs={{0,64},{32,224},{64,128},{96,32},{128,192},{160,96},{192,0},{224,1... | collective-permute-start | bytes 589832 | tf_op jit(solution)/shard_map/ppermute | solution.py:238
  39.4 0.2 collective-permute-done.3.came_ref
  39.6 4.3 %collective-permute-done.4 = bf16[8,96,128]{2,1,0:T(8,128)(2,1)S(1)} collective-permute-done((bf16[8,96,128]{2,1,0:T(8,128)(2,1)S(1)}, bf16[8,96,128]{2,1,0:T(8,128)(2,1)S(1)}, u32[]{:S(2)}, u32[]{:S(2)}) %collective-permute-start.4) | collective-permute-done | bytes 196640 | tf_op jit(solution)/shard_map/ppermute | solution.py:238
  44.0 0.0 copy-done.2
  44.0 0.8 %add_convert_fusion = bf16[8,96,128]{2,1,0:T(8,128)(2,1)} fusion(f32[8,96,128]{2,1,0:T(8,128)S(1)} %presum.1, bf16[8,96,128]{2,1,0:T(8,128)(2,1)S(1)} %collective-permute-done.4, f32[128]{0:T(128)S(1)} %copy-done.2), kind=kLoop, calls=%fused_computation | loop fusion | flops 491520 | bytes 786944 | tf_op jit(solution)/shard_map/convert_element_type | solution.py:268
  (3 shorter events, 0.1 us)
Async XLA Ops:
  0.0 9.7 %copy-start = (bf16[128,96,32]{0,2,1:T(8,128)(2,1)S(1)}, bf16[128,96,32]{0,2,1:T(8,128)(2,1)}, u32[]{:S(2)}) copy-start(bf16[128,96,32]{0,2,1:T(8,128)(2,1)} %param.5) | copy-start | bytes 2359300
  1.7 17.6 %all-to-all-start = ((bf16[32,2,32,128]{3,2,1,0:T(8,128)(2,1)}), bf16[32,2,32,128]{3,2,1,0:T(8,128)(2,1)S(1)}, u32[]{:S(2)}, u32[]{:S(2)}) async-start(bf16[32,2,32,128]{3,2,1,0:T(8,128)(2,1)} %spread.1), calls=%async_computation | async-start | bytes 1048576 | tf_op jit(solution)/shard_map/all_to_all | solution.py:248
  9.7 3.2 %collective-permute-start = (bf16[96,32,128]{2,1,0:T(8,128)(2,1)S(1)}, bf16[96,32,128]{2,1,0:T(8,128)(2,1)S(1)}, u32[]{:S(2)}, u32[]{:S(2)}) collective-permute-start(bf16[96,32,128]{2,1,0:T(8,128)(2,1)S(1)} %bitcast.11), channel_id=1, source_target_pairs={{0,32},{32,0},{1,33},{33,1},{2,34},{34,2},{3,35},{35,3},{4,36},{36... | collective-permute-start | bytes 2359304 | tf_op jit(solution)/shard_map/ppermute | solution.py:247
  19.3 2.4 %copy-start.1 = (bf16[1024,128]{1,0:T(8,128)(2,1)S(1)}, bf16[1024,128]{1,0:T(8,128)(2,1)}, u32[]{:S(2)}) copy-start(bf16[1024,128]{1,0:T(8,128)(2,1)} %matrix_ref.1) | copy-start | bytes 786436
  19.3 3.5 %collective-permute-start.1 = (bf16[4,8,32,128]{3,2,1,0:T(8,128)(2,1)S(1)}, bf16[4,8,32,128]{3,2,1,0:T(8,128)(2,1)S(1)}, u32[]{:S(2)}, u32[]{:S(2)}) collective-permute-start(bf16[4,8,32,128]{3,2,1,0:T(8,128)(2,1)S(1)} %select.1), channel_id=1, source_target_pairs={{0,32},{32,0},{1,33},{33,1},{2,34},{34,2},{3,35},{35,3},{4,36},{36... | collective-permute-start | bytes 786440 | tf_op jit(solution)/shard_map/ppermute | solution.py:255
  24.0 11.3 %collective-permute-start.2 = (bf16[8,96,128]{2,1,0:T(8,128)(2,1)S(1)}, bf16[8,96,128]{2,1,0:T(8,128)(2,1)S(1)}, u32[]{:S(2)}, u32[]{:S(2)}) collective-permute-start(bf16[8,96,128]{2,1,0:T(8,128)(2,1)S(1)} %pair_block.4), channel_id=1, source_target_pairs={{0,64},{32,224},{64,128},{96,32},{128,192},{160,96},{192,0},{224,1... | collective-permute-start | bytes 589832 | tf_op jit(solution)/shard_map/ppermute | solution.py:238
  30.3 9.3 %collective-permute-start.3 = (bf16[8,96,128]{2,1,0:T(8,128)(2,1)S(1)}, bf16[8,96,128]{2,1,0:T(8,128)(2,1)S(1)}, u32[]{:S(2)}, u32[]{:S(2)}) collective-permute-start(bf16[8,96,128]{2,1,0:T(8,128)(2,1)S(1)} %pair_block.7), channel_id=1, source_target_pairs={{0,96},{32,192},{64,160},{96,0},{128,224},{160,64},{192,32},{224,1... | collective-permute-start | bytes 589832 | tf_op jit(solution)/shard_map/ppermute | solution.py:238
  35.3 8.7 %copy-start.2 = (f32[128]{0:T(128)S(1)}, f32[128]{0:T(128)}, u32[]{:S(2)}) copy-start(f32[128]{0:T(128)} %param.7) | copy-start | bytes 1540
  35.3 8.7 %collective-permute-start.4 = (bf16[8,96,128]{2,1,0:T(8,128)(2,1)S(1)}, bf16[8,96,128]{2,1,0:T(8,128)(2,1)S(1)}, u32[]{:S(2)}, u32[]{:S(2)}) collective-permute-start(bf16[8,96,128]{2,1,0:T(8,128)(2,1)S(1)} %merge.1), channel_id=1, source_target_pairs={{0,64},{32,224},{64,128},{96,32},{128,192},{160,96},{192,0},{224,1... | collective-permute-start | bytes 589832 | tf_op jit(solution)/shard_map/ppermute | solution.py:238

commit v7 on v6

--- a/solution.py
+++ b/solution.py
@@ -29,22 +29,16 @@
     return pl.CostEstimate(flops=flops, bytes_accessed=nbytes, transcendentals=0)
 
 
-def spread_kernel(in_ref, out_ref, held_ref, filled_ref, in_sem, out_sems):
+def spread_kernel(in_ref, out_ref, held_ref, filled_ref, in_sem, out_sem):
     fetch = pltpu.make_async_copy(in_ref, held_ref, in_sem)
     fetch.start()
     fetch.wait()
     own = held_ref[...]
-    each = filled_ref.shape[0]
-    for t in range(each):
+    for t in range(TILES):
         filled_ref[t] = own
-    copies = [
-        pltpu.make_async_copy(filled_ref, out_ref.at[pl.ds(i * each, each)], out_sems.at[i])
-        for i in range(TILES // each)
-    ]
-    for copy in copies:
-        copy.start()
-    for copy in copies:
-        copy.wait()
+    store = pltpu.make_async_copy(filled_ref, out_ref, out_sem)
+    store.start()
+    store.wait()
 
 
 def spread(own):
@@ -55,9 +49,9 @@
         out_specs=ANY,
         scratch_shapes=[
             pltpu.VMEM(own.shape, jnp.bfloat16),
-            pltpu.VMEM((8,) + own.shape, jnp.bfloat16),
+            pltpu.VMEM((TILES,) + own.shape, jnp.bfloat16),
             pltpu.SemaphoreType.DMA,
-            pltpu.SemaphoreType.DMA((TILES // 8,)),
+            pltpu.SemaphoreType.DMA,
         ],
         compiler_params=limit(60),
         cost_estimate=cost(1 << 20),
@@ -161,13 +155,12 @@
                     r * FEATS:(r + 1) * FEATS, f * LANES:(f + 1) * LANES
                 ]
     cols = out_ref.shape[1]
-    for r in range(0, ROWS, 4):
+    for r in range(0, ROWS, 2):
         mixed = jnp.dot(
-            w_ref[...], stack_ref[:, r * LANES:(r + 4) * LANES], preferred_element_type=jnp.float32
+            w_ref[...], stack_ref[:, r * LANES:(r + 2) * LANES], preferred_element_type=jnp.float32
         )
-        for i in range(4):
-            lanes = slice(i * LANES, (i + 1) * LANES)
-            out_ref[r + i] = mixed[:, lanes].T[:cols].astype(out_ref.dtype)
+        out_ref[r] = mixed[:, :LANES].T[:cols].astype(out_ref.dtype)
+        out_ref[r + 1] = mixed[:, LANES:].T[:cols].astype(out_ref.dtype)
 
 
 def pair_block(slot, own, other, b_own, b_other, wt, cols, dtype=jnp.bfloat16):
@@ -178,7 +171,7 @@
         out_specs=WHOLE,
         scratch_shapes=[pltpu.VMEM((FEATS * FEATS, ROWS * LANES), jnp.bfloat16)],
         compiler_params=limit(16),
-        cost_estimate=cost(4 << 20, 3 << 30),
+        cost_estimate=cost(1 << 16, 1 << 24),
         name="pair_block",
     )(own, other, b_own, b_other, wt)
 
@@ -260,7 +253,7 @@
     left_part = block(NEAR, dtype=jnp.float32)
     right = send(block(CROSS), (1, 3), 1)
     kept = block(KEPT, dtype=jnp.float32)
-    far, kept, left_part = lax.optimization_barrier((far, kept, left_part))
+    far, left_part = lax.optimization_barrier((far, left_part))
     merged = add_to(left_part, far, jnp.bfloat16, "merge", 200 << 20)
     left = send(merged, (1, 3))
     presum = add_to(kept, right, jnp.float32, "presum", 200 << 20)

time: 45.5 us -> 45.6 us (level)
  transfers between devices with their start and end apart: 6 -> 6, of which waited for: 6 -> 5; matrix products, arithmetic and copies ran while one was open for 0% -> 0% of each run, Pallas kernels for 14% -> 14%
where the time goes in v7:
time: 45.6 us; the launch traced here: 44.8 us
  starting transfers between devices  21.4 us (47%)
  waiting for transfers between devices  13.4 us (29%)
  Pallas kernels  9.13 us (20%)
  other arithmetic  0.75 us (2%)
    ppermute x3, starting transfers between devices, send(): return lax.ppermute(part, DEPTH_AXES, pairs)  9.65 us
    all_to_all x1, starting transfers between devices, local(): lax.all_to_all(copies, TILE_AXES, split_axis=0, concat_axis=0, tiled=True)  8.01 us
    ppermute x3, waiting for transfers between devices, send(): return lax.ppermute(part, DEPTH_AXES, pairs)  6.67 us
    all_to_all x1, waiting for transfers between devices, local(): lax.all_to_all(copies, TILE_AXES, split_axis=0, concat_axis=0, tiled=True)  5.21 us
    pallas_call x4, Pallas kernels, pair_block(): pl.pallas_call(functools.partial(pair_kernel, slot), out_shape=jax.ShapeD...  4.68 us
    ppermute x1, starting transfers between devices, local(): a_other = lax.ppermute(a_give, 'core', SWAP)  2.38 us
    pallas_call x2, Pallas kernels, turn_factor(): pl.pallas_call(turn_kernel, out_shape=jax.ShapeDtypeStruct((LANES, FEATS...  2.24 us
    pallas_call x1, Pallas kernels, spread(): pl.pallas_call(spread_kernel, out_shape=jax.ShapeDtypeStruct((TILES,) + o...  1.72 us
  transfers between devices with their start and end apart: 6, of which 5 were waited for; matrix products, arithmetic and copies ran while one was open for 0% of the time, Pallas kernels for 14%

profile of v7, /device:TPU:33, one launch (start us, length us, event | category | flops | bytes accessed | tf_op | source)
XLA Modules:
  0.0 44.8 jit_solution(3937128803025069857)
XLA Ops:
  0.0 0.0 copy-start
  0.0 1.7 %spread.1 = bf16[32,2,32,128]{3,2,1,0:T(8,128)(2,1)} custom-call(bf16[2,32,128]{2,1,0:T(8,128)(2,1)} %bitcast.14), custom_call_target="tpu_custom_call" | custom-call | bytes 1048576 | tf_op jit(solution)/shard_map/spread/pallas_call | solution.py:45
  1.7 8.0 %all-to-all-start = ((bf16[32,2,32,128]{3,2,1,0:T(8,128)(2,1)}), bf16[32,2,32,128]{3,2,1,0:T(8,128)(2,1)S(1)}, u32[]{:S(2)}, u32[]{:S(2)}) async-start(bf16[32,2,32,128]{3,2,1,0:T(8,128)(2,1)} %spread.1), calls=%async_computation | async-start | bytes 1048576 | tf_op jit(solution)/shard_map/all_to_all | solution.py:241
  9.7 0.0 copy-done
  9.8 1.3 %collective-permute-start = (bf16[96,32,128]{2,1,0:T(8,128)(2,1)S(1)}, bf16[96,32,128]{2,1,0:T(8,128)(2,1)S(1)}, u32[]{:S(2)}, u32[]{:S(2)}) collective-permute-start(bf16[96,32,128]{2,1,0:T(8,128)(2,1)S(1)} %bitcast.11), channel_id=1, source_target_pairs={{0,32},{32,0},{1,33},{33,1},{2,34},{34,2},{3,35},{35,3},{4,36},{36... | collective-permute-start | bytes 2359304 | tf_op jit(solution)/shard_map/ppermute | solution.py:240
  11.1 1.1 %turn_factor.3.b_own_ref = bf16[128,4096]{1,0:T(8,128)(2,1)S(1)} custom-call(bf16[3072,128]{1,0:T(8,128)(2,1)S(1)} %bitcast.12), custom_call_target="tpu_custom_call" | custom-call | bytes 4194304 | tf_op jit(solution)/shard_map/turn_factor/pallas_call | solution.py:100
  12.2 0.8 %collective-permute-done = bf16[96,32,128]{2,1,0:T(8,128)(2,1)S(1)} collective-permute-done((bf16[96,32,128]{2,1,0:T(8,128)(2,1)S(1)}, bf16[96,32,128]{2,1,0:T(8,128)(2,1)S(1)}, u32[]{:S(2)}, u32[]{:S(2)}) %collective-permute-start) | collective-permute-done | bytes 786464 | tf_op jit(solution)/shard_map/ppermute | solution.py:240
  13.0 1.1 %turn_factor.2.b_other_ref = bf16[128,4096]{1,0:T(8,128)(2,1)S(1)} custom-call(bf16[3072,128]{1,0:T(8,128)(2,1)S(1)} %bitcast.13), custom_call_target="tpu_custom_call" | custom-call | bytes 4194304 | tf_op jit(solution)/shard_map/turn_factor/pallas_call | solution.py:100
  14.1 5.2 %all-to-all-done = bf16[32,2,32,128]{3,2,1,0:T(8,128)(2,1)S(1)} async-done(((bf16[32,2,32,128]{3,2,1,0:T(8,128)(2,1)}), bf16[32,2,32,128]{3,2,1,0:T(8,128)(2,1)S(1)}, u32[]{:S(2)}, u32[]{:S(2)}) %all-to-all-start) | async-done | bytes 524320 | tf_op jit(solution)/shard_map/all_to_all | solution.py:241
  19.3 0.0 copy-start.1
  19.4 2.4 %collective-permute-start.1 = (bf16[4,8,32,128]{3,2,1,0:T(8,128)(2,1)S(1)}, bf16[4,8,32,128]{3,2,1,0:T(8,128)(2,1)S(1)}, u32[]{:S(2)}, u32[]{:S(2)}) collective-permute-start(bf16[4,8,32,128]{3,2,1,0:T(8,128)(2,1)S(1)} %select.1), channel_id=1, source_target_pairs={{0,32},{32,0},{1,33},{33,1},{2,34},{34,2},{3,35},{35,3},{4,36},{36... | collective-permute-start | bytes 786440 | tf_op jit(solution)/shard_map/ppermute | solution.py:248
  21.7 0.0 copy-done.1
  21.7 0.4 turn_matrix.1.w_ref
  22.1 0.8 %collective-permute-done.1.other_ref = bf16[4,8,32,128]{3,2,1,0:T(8,128)(2,1)S(1)} collective-permute-done((bf16[4,8,32,128]{3,2,1,0:T(8,128)(2,1)S(1)}, bf16[4,8,32,128]{3,2,1,0:T(8,128)(2,1)S(1)}, u32[]{:S(2)}, u32[]{:S(2)}) %collective-permute-start.1) | collective-permute-done | bytes 262176 | tf_op jit(solution)/shard_map/ppermute | solution.py:248
  22.9 1.1 %pair_block.6 = bf16[8,96,128]{2,1,0:T(8,128)(2,1)S(1)} custom-call(bf16[4,2,8,32,128]{4,3,2,1,0:T(8,128)(2,1)S(1)} %bitcast.7, bf16[4,8,32,128]{3,2,1,0:T(8,128)(2,1)S(1)} %collective-permute-done.1.other_ref, bf16[128,4096]{1,0:T(8,128)(2,1)S(1)} %turn_factor.3.b_own_ref, bf16[128,4096]{1,0:T(8,128)(2,1)S(1)} %turn_factor.2.b_other_ref, ...), custom_call_target="tpu_custom_call" | custom-call | flops 16777216 | bytes 65536 | tf_op jit(solution)/shard_map/pair_block/pallas_call | solution.py:167
  24.0 5.2 %collective-permute-start.3 = (bf16[8,96,128]{2,1,0:T(8,128)(2,1)S(1)}, bf16[8,96,128]{2,1,0:T(8,128)(2,1)S(1)}, u32[]{:S(2)}, u32[]{:S(2)}) collective-permute-start(bf16[8,96,128]{2,1,0:T(8,128)(2,1)S(1)} %pair_block.6), channel_id=1, source_target_pairs={{0,64},{32,224},{64,128},{96,32},{128,192},{160,96},{192,0},{224,1... | collective-permute-start | bytes 589832 | tf_op jit(solution)/shard_map/ppermute | solution.py:231
  29.2 1.1 %pair_block.5 = bf16[8,96,128]{2,1,0:T(8,128)(2,1)S(1)} custom-call(bf16[4,2,8,32,128]{4,3,2,1,0:T(8,128)(2,1)S(1)} %bitcast.8, bf16[4,8,32,128]{3,2,1,0:T(8,128)(2,1)S(1)} %collective-permute-done.1.other_ref, bf16[128,4096]{1,0:T(8,128)(2,1)S(1)} %turn_factor.3.b_own_ref, bf16[128,4096]{1,0:T(8,128)(2,1)S(1)} %turn_factor.2.b_other_ref, ...), custom_call_target="tpu_custom_call" | custom-call | flops 16777216 | bytes 65536 | tf_op jit(solution)/shard_map/pair_block/pallas_call | solution.py:167
  30.4 0.4 collective-permute-start.2
  30.7 1.2 %pair_block.7.kept_ref = f32[8,96,128]{2,1,0:T(8,128)S(1)} custom-call(bf16[4,2,8,32,128]{4,3,2,1,0:T(8,128)(2,1)S(1)} %bitcast.9, bf16[4,8,32,128]{3,2,1,0:T(8,128)(2,1)S(1)} %collective-permute-done.1.other_ref, bf16[128,4096]{1,0:T(8,128)(2,1)S(1)} %turn_factor.3.b_own_ref, bf16[128,4096]{1,0:T(8,128)(2,1)S(1)} %turn_factor.2.b_other_ref, ...), custom_call_target="tpu_custom_call" | custom-call | flops 16777216 | bytes 65536 | tf_op jit(solution)/shard_map/pair_block/pallas_call | solution.py:167
  31.9 3.4 %collective-permute-done.3.came_ref = bf16[8,96,128]{2,1,0:T(8,128)(2,1)S(1)} collective-permute-done((bf16[8,96,128]{2,1,0:T(8,128)(2,1)S(1)}, bf16[8,96,128]{2,1,0:T(8,128)(2,1)S(1)}, u32[]{:S(2)}, u32[]{:S(2)}) %collective-permute-start.3) | collective-permute-done | bytes 196640 | tf_op jit(solution)/shard_map/ppermute | solution.py:231
  35.4 4.1 %collective-permute-start.4 = (bf16[8,96,128]{2,1,0:T(8,128)(2,1)S(1)}, bf16[8,96,128]{2,1,0:T(8,128)(2,1)S(1)}, u32[]{:S(2)}, u32[]{:S(2)}) collective-permute-start(bf16[8,96,128]{2,1,0:T(8,128)(2,1)S(1)} %merge.1), channel_id=1, source_target_pairs={{0,64},{32,224},{64,128},{96,32},{128,192},{160,96},{192,0},{224,1... | collective-permute-start | bytes 589832 | tf_op jit(solution)/shard_map/ppermute | solution.py:231
  39.5 1.2 %pair_block.4.kept_ref = f32[8,96,128]{2,1,0:T(8,128)S(1)} custom-call(bf16[4,2,8,32,128]{4,3,2,1,0:T(8,128)(2,1)S(1)} %bitcast.10, bf16[4,8,32,128]{3,2,1,0:T(8,128)(2,1)S(1)} %collective-permute-done.1.other_ref, bf16[128,4096]{1,0:T(8,128)(2,1)S(1)} %turn_factor.3.b_own_ref, bf16[128,4096]{1,0:T(8,128)(2,1)S(1)} %turn_factor.2.b_other_ref, ...), custom_call_target="tpu_custom_call" | custom-call | flops 16777216 | bytes 65536 | tf_op jit(solution)/shard_map/pair_block/pallas_call | solution.py:167
  40.7 0.0 copy-start.2
  40.7 0.0 collective-permute-done.2.came_ref
  40.8 3.3 %collective-permute-done.4 = bf16[8,96,128]{2,1,0:T(8,128)(2,1)S(1)} collective-permute-done((bf16[8,96,128]{2,1,0:T(8,128)(2,1)S(1)}, bf16[8,96,128]{2,1,0:T(8,128)(2,1)S(1)}, u32[]{:S(2)}, u32[]{:S(2)}) %collective-permute-start.4) | collective-permute-done | bytes 196640 | tf_op jit(solution)/shard_map/ppermute | solution.py:231
  44.0 0.0 copy-done.2
  44.0 0.8 %add_convert_fusion = bf16[8,96,128]{2,1,0:T(8,128)(2,1)} fusion(f32[8,96,128]{2,1,0:T(8,128)S(1)} %presum.1, bf16[8,96,128]{2,1,0:T(8,128)(2,1)S(1)} %collective-permute-done.4, f32[128]{0:T(128)S(1)} %copy-done.2), kind=kLoop, calls=%fused_computation | loop fusion | flops 491520 | bytes 786944 | tf_op jit(solution)/shard_map/convert_element_type | solution.py:261
  (3 shorter events, 0.1 us)
Async XLA Ops:
  0.0 9.7 %copy-start = (bf16[128,96,32]{0,2,1:T(8,128)(2,1)S(1)}, bf16[128,96,32]{0,2,1:T(8,128)(2,1)}, u32[]{:S(2)}) copy-start(bf16[128,96,32]{0,2,1:T(8,128)(2,1)} %param.5) | copy-start | bytes 2359300
  1.7 17.6 %all-to-all-start = ((bf16[32,2,32,128]{3,2,1,0:T(8,128)(2,1)}), bf16[32,2,32,128]{3,2,1,0:T(8,128)(2,1)S(1)}, u32[]{:S(2)}, u32[]{:S(2)}) async-start(bf16[32,2,32,128]{3,2,1,0:T(8,128)(2,1)} %spread.1), calls=%async_computation | async-start | bytes 1048576 | tf_op jit(solution)/shard_map/all_to_all | solution.py:241
  9.8 3.2 %collective-permute-start = (bf16[96,32,128]{2,1,0:T(8,128)(2,1)S(1)}, bf16[96,32,128]{2,1,0:T(8,128)(2,1)S(1)}, u32[]{:S(2)}, u32[]{:S(2)}) collective-permute-start(bf16[96,32,128]{2,1,0:T(8,128)(2,1)S(1)} %bitcast.11), channel_id=1, source_target_pairs={{0,32},{32,0},{1,33},{33,1},{2,34},{34,2},{3,35},{35,3},{4,36},{36... | collective-permute-start | bytes 2359304 | tf_op jit(solution)/shard_map/ppermute | solution.py:240
  19.3 2.4 %copy-start.1 = (bf16[1024,128]{1,0:T(8,128)(2,1)S(1)}, bf16[1024,128]{1,0:T(8,128)(2,1)}, u32[]{:S(2)}) copy-start(bf16[1024,128]{1,0:T(8,128)(2,1)} %matrix_ref.1) | copy-start | bytes 786436
  19.4 3.5 %collective-permute-start.1 = (bf16[4,8,32,128]{3,2,1,0:T(8,128)(2,1)S(1)}, bf16[4,8,32,128]{3,2,1,0:T(8,128)(2,1)S(1)}, u32[]{:S(2)}, u32[]{:S(2)}) collective-permute-start(bf16[4,8,32,128]{3,2,1,0:T(8,128)(2,1)S(1)} %select.1), channel_id=1, source_target_pairs={{0,32},{32,0},{1,33},{33,1},{2,34},{34,2},{3,35},{35,3},{4,36},{36... | collective-permute-start | bytes 786440 | tf_op jit(solution)/shard_map/ppermute | solution.py:248
  24.0 11.3 %collective-permute-start.3 = (bf16[8,96,128]{2,1,0:T(8,128)(2,1)S(1)}, bf16[8,96,128]{2,1,0:T(8,128)(2,1)S(1)}, u32[]{:S(2)}, u32[]{:S(2)}) collective-permute-start(bf16[8,96,128]{2,1,0:T(8,128)(2,1)S(1)} %pair_block.6), channel_id=1, source_target_pairs={{0,64},{32,224},{64,128},{96,32},{128,192},{160,96},{192,0},{224,1... | collective-permute-start | bytes 589832 | tf_op jit(solution)/shard_map/ppermute | solution.py:231
  30.4 10.3 %collective-permute-start.2 = (bf16[8,96,128]{2,1,0:T(8,128)(2,1)S(1)}, bf16[8,96,128]{2,1,0:T(8,128)(2,1)S(1)}, u32[]{:S(2)}, u32[]{:S(2)}) collective-permute-start(bf16[8,96,128]{2,1,0:T(8,128)(2,1)S(1)} %pair_block.5), channel_id=1, source_target_pairs={{0,96},{32,192},{64,160},{96,0},{128,224},{160,64},{192,32},{224,1... | collective-permute-start | bytes 589832 | tf_op jit(solution)/shard_map/ppermute | solution.py:231
  35.4 8.7 %collective-permute-start.4 = (bf16[8,96,128]{2,1,0:T(8,128)(2,1)S(1)}, bf16[8,96,128]{2,1,0:T(8,128)(2,1)S(1)}, u32[]{:S(2)}, u32[]{:S(2)}) collective-permute-start(bf16[8,96,128]{2,1,0:T(8,128)(2,1)S(1)} %merge.1), channel_id=1, source_target_pairs={{0,64},{32,224},{64,128},{96,32},{128,192},{160,96},{192,0},{224,1... | collective-permute-start | bytes 589832 | tf_op jit(solution)/shard_map/ppermute | solution.py:231
  40.7 3.4 %copy-start.2 = (f32[128]{0:T(128)S(1)}, f32[128]{0:T(128)}, u32[]{:S(2)}) copy-start(f32[128]{0:T(128)} %param.7) | copy-start | bytes 1540

commit v8 on v7

--- a/solution.py
+++ b/solution.py
@@ -113,7 +113,7 @@
     zh = lax.axis_index("zh")
     core = 1 - lax.axis_index("core")
     for slot, (hops, flip) in enumerate(BLOCKS):
-        block = (zh + jnp.where(core == 0, hops[0], hops[1])) & (RING - 1)
+        block = (zh + jnp.where((core + lax.axis_index("zl")) & 1 == 0, hops[0], hops[1])) & (RING - 1)
         out_ref[slot] = in_ref[block, 1 - core if flip else core]
 
 
@@ -133,7 +133,7 @@
     zh = lax.axis_index("zh")
     core = lax.axis_index("core")
     hops, flip = BLOCKS[slot]
-    block = (zh + jnp.where(core == 0, hops[0], hops[1])) & (RING - 1)
+    block = (zh + jnp.where((core + lax.axis_index("zl")) & 1 == 0, hops[0], hops[1])) & (RING - 1)
     half = 1 - core if flip else core
     width = ROWS * FEATS
     a = jnp.concatenate(
@@ -171,7 +171,7 @@
         out_specs=WHOLE,
         scratch_shapes=[pltpu.VMEM((FEATS * FEATS, ROWS * LANES), jnp.bfloat16)],
         compiler_params=limit(16),
-        cost_estimate=cost(1 << 16, 1 << 24),
+        cost_estimate=cost(4 << 20, 3 << 30),
         name="pair_block",
     )(own, other, b_own, b_other, wt)
 
@@ -227,8 +227,10 @@
     pairs = []
     for z in range(RING):
         for c in range(2):
-            pairs.append((z * 2 + c, (z + hops[c]) % RING * 2 + (c ^ flip)))
-    return lax.ppermute(part, DEPTH_AXES, pairs)
+            for low in range(2):
+                to = (z + hops[c ^ low]) % RING
+                pairs.append(((z * 2 + c) * 2 + low, (to * 2 + (c ^ flip)) * 2 + low))
+    return lax.ppermute(part, DEPTH_AXES + ("zl",), pairs)
 
 
 def local(first, second, matrix, bias):
@@ -253,7 +255,7 @@
     left_part = block(NEAR, dtype=jnp.float32)
     right = send(block(CROSS), (1, 3), 1)
     kept = block(KEPT, dtype=jnp.float32)
-    far, left_part = lax.optimization_barrier((far, left_part))
+    far, kept, left_part = lax.optimization_barrier((far, kept, left_part))
     merged = add_to(left_part, far, jnp.bfloat16, "merge", 200 << 20)
     left = send(merged, (1, 3))
     presum = add_to(kept, right, jnp.float32, "presum", 200 << 20)

time: 45.6 us -> 45.7 us (level)
  the two profiles are of different devices: /device:TPU:33 before, /device:TPU:2 now
where the time goes in v8:
time: 45.7 us; the launch traced here: 45.4 us
  waiting for transfers between devices  21.9 us (48%)
  starting transfers between devices  12.7 us (28%)
  Pallas kernels  9.14 us (20%)
  local copies, waits for them, and re-layouts  0.84 us (2%)
  other arithmetic  0.75 us (2%)
    ppermute x3, waiting for transfers between devices, send(): return lax.ppermute(part, DEPTH_AXES + ('zl',), pairs)  13.6 us
    all_to_all x1, starting transfers between devices, local(): lax.all_to_all(copies, TILE_AXES, split_axis=0, concat_axis=0, tiled=True)  8.98 us
    all_to_all x1, waiting for transfers between devices, local(): lax.all_to_all(copies, TILE_AXES, split_axis=0, concat_axis=0, tiled=True)  6.82 us
    pallas_call x4, Pallas kernels, pair_block(): pl.pallas_call(functools.partial(pair_kernel, slot), out_shape=jax.ShapeD...  4.69 us
    ppermute x3, starting transfers between devices, send(): return lax.ppermute(part, DEPTH_AXES + ('zl',), pairs)  3.52 us
    pallas_call x2, Pallas kernels, turn_factor(): pl.pallas_call(turn_kernel, out_shape=jax.ShapeDtypeStruct((LANES, FEATS...  2.24 us
    pallas_call x1, Pallas kernels, spread(): pl.pallas_call(spread_kernel, out_shape=jax.ShapeDtypeStruct((TILES,) + o...  1.72 us
    ppermute x1, waiting for transfers between devices, local(): b_swapped = lax.ppermute(bt, 'core', SWAP)  1.15 us
  transfers between devices with their start and end apart: 6, of which 5 were waited for; matrix products, arithmetic and copies ran while one was open for 0% of the time, Pallas kernels for 14%

profile of v8, /device:TPU:2, one launch (start us, length us, event | category | flops | bytes accessed | tf_op | source)
XLA Modules:
  0.0 45.4 jit_solution(2382648153210550694)
XLA Ops:
  0.0 0.0 copy-start
  0.0 1.7 %spread.1 = bf16[32,2,32,128]{3,2,1,0:T(8,128)(2,1)} custom-call(bf16[2,32,128]{2,1,0:T(8,128)(2,1)} %bitcast.14), custom_call_target="tpu_custom_call" | custom-call | bytes 1048576 | tf_op jit(solution)/shard_map/spread/pallas_call | solution.py:45
  1.7 9.0 %all-to-all-start = ((bf16[32,2,32,128]{3,2,1,0:T(8,128)(2,1)}), bf16[32,2,32,128]{3,2,1,0:T(8,128)(2,1)S(1)}, u32[]{:S(2)}, u32[]{:S(2)}) async-start(bf16[32,2,32,128]{3,2,1,0:T(8,128)(2,1)} %spread.1), calls=%async_computation | async-start | bytes 1048576 | tf_op jit(solution)/shard_map/all_to_all | solution.py:243
  10.7 0.0 copy-done
  10.7 0.1 collective-permute-start
  10.8 1.1 %turn_factor.3.b_own_ref = bf16[128,4096]{1,0:T(8,128)(2,1)S(1)} custom-call(bf16[3072,128]{1,0:T(8,128)(2,1)S(1)} %bitcast.12), custom_call_target="tpu_custom_call" | custom-call | bytes 4194304 | tf_op jit(solution)/shard_map/turn_factor/pallas_call | solution.py:100
  12.0 1.1 %collective-permute-done = bf16[96,32,128]{2,1,0:T(8,128)(2,1)S(1)} collective-permute-done((bf16[96,32,128]{2,1,0:T(8,128)(2,1)S(1)}, bf16[96,32,128]{2,1,0:T(8,128)(2,1)S(1)}, u32[]{:S(2)}, u32[]{:S(2)}) %collective-permute-start) | collective-permute-done | bytes 786464 | tf_op jit(solution)/shard_map/ppermute | solution.py:242
  13.1 1.1 %turn_factor.2.b_other_ref = bf16[128,4096]{1,0:T(8,128)(2,1)S(1)} custom-call(bf16[3072,128]{1,0:T(8,128)(2,1)S(1)} %bitcast.13), custom_call_target="tpu_custom_call" | custom-call | bytes 4194304 | tf_op jit(solution)/shard_map/turn_factor/pallas_call | solution.py:100
  14.2 6.8 %all-to-all-done = bf16[32,2,32,128]{3,2,1,0:T(8,128)(2,1)S(1)} async-done(((bf16[32,2,32,128]{3,2,1,0:T(8,128)(2,1)}), bf16[32,2,32,128]{3,2,1,0:T(8,128)(2,1)S(1)}, u32[]{:S(2)}, u32[]{:S(2)}) %all-to-all-start) | async-done | bytes 524320 | tf_op jit(solution)/shard_map/all_to_all | solution.py:243
  21.0 0.0 copy-start.1
  21.1 0.1 collective-permute-start.1
  21.2 0.8 %copy-done.1 = bf16[1024,128]{1,0:T(8,128)(2,1)S(1)} copy-done((bf16[1024,128]{1,0:T(8,128)(2,1)S(1)}, bf16[1024,128]{1,0:T(8,128)(2,1)}, u32[]{:S(2)}) %copy-start.1) | copy-done | bytes 262168
  22.0 0.4 turn_matrix.1.w_ref
  22.4 0.3 collective-permute-done.1.other_ref
  22.7 1.1 %pair_block.4 = bf16[8,96,128]{2,1,0:T(8,128)(2,1)S(1)} custom-call(bf16[4,2,8,32,128]{4,3,2,1,0:T(8,128)(2,1)S(1)} %bitcast.7, bf16[4,8,32,128]{3,2,1,0:T(8,128)(2,1)S(1)} %collective-permute-done.1.other_ref, bf16[128,4096]{1,0:T(8,128)(2,1)S(1)} %turn_factor.3.b_own_ref, bf16[128,4096]{1,0:T(8,128)(2,1)S(1)} %turn_factor.2.b_other_ref, ...), custom_call_target="tpu_custom_call" | custom-call | flops 3221225472 | bytes 4194304 | tf_op jit(solution)/shard_map/pair_block/pallas_call | solution.py:167
  23.8 3.3 %collective-permute-start.2 = (bf16[8,96,128]{2,1,0:T(8,128)(2,1)S(1)}, bf16[8,96,128]{2,1,0:T(8,128)(2,1)S(1)}, u32[]{:S(2)}, u32[]{:S(2)}) collective-permute-start(bf16[8,96,128]{2,1,0:T(8,128)(2,1)S(1)} %pair_block.4), channel_id=1, source_target_pairs={{0,64},{16,208},{32,224},{48,112},{64,128},{80,16},{96,32},{112,17... | collective-permute-start | bytes 589832 | tf_op jit(solution)/shard_map/ppermute | solution.py:233
  27.2 1.1 %pair_block.7 = bf16[8,96,128]{2,1,0:T(8,128)(2,1)S(1)} custom-call(bf16[4,2,8,32,128]{4,3,2,1,0:T(8,128)(2,1)S(1)} %bitcast.8, bf16[4,8,32,128]{3,2,1,0:T(8,128)(2,1)S(1)} %collective-permute-done.1.other_ref, bf16[128,4096]{1,0:T(8,128)(2,1)S(1)} %turn_factor.3.b_own_ref, bf16[128,4096]{1,0:T(8,128)(2,1)S(1)} %turn_factor.2.b_other_ref, ...), custom_call_target="tpu_custom_call" | custom-call | flops 3221225472 | bytes 4194304 | tf_op jit(solution)/shard_map/pair_block/pallas_call | solution.py:167
  28.3 0.1 collective-permute-start.3
  28.4 1.2 %pair_block.6.kept_ref = f32[8,96,128]{2,1,0:T(8,128)S(1)} custom-call(bf16[4,2,8,32,128]{4,3,2,1,0:T(8,128)(2,1)S(1)} %bitcast.9, bf16[4,8,32,128]{3,2,1,0:T(8,128)(2,1)S(1)} %collective-permute-done.1.other_ref, bf16[128,4096]{1,0:T(8,128)(2,1)S(1)} %turn_factor.3.b_own_ref, bf16[128,4096]{1,0:T(8,128)(2,1)S(1)} %turn_factor.2.b_other_ref, ...), custom_call_target="tpu_custom_call" | custom-call | flops 3221225472 | bytes 4194304 | tf_op jit(solution)/shard_map/pair_block/pallas_call | solution.py:167
  29.6 1.2 %pair_block.5.kept_ref = f32[8,96,128]{2,1,0:T(8,128)S(1)} custom-call(bf16[4,2,8,32,128]{4,3,2,1,0:T(8,128)(2,1)S(1)} %bitcast.10, bf16[4,8,32,128]{3,2,1,0:T(8,128)(2,1)S(1)} %collective-permute-done.1.other_ref, bf16[128,4096]{1,0:T(8,128)(2,1)S(1)} %turn_factor.3.b_own_ref, bf16[128,4096]{1,0:T(8,128)(2,1)S(1)} %turn_factor.2.b_other_ref, ...), custom_call_target="tpu_custom_call" | custom-call | flops 3221225472 | bytes 4194304 | tf_op jit(solution)/shard_map/pair_block/pallas_call | solution.py:167
  30.9 5.9 %collective-permute-done.2.came_ref = bf16[8,96,128]{2,1,0:T(8,128)(2,1)S(1)} collective-permute-done((bf16[8,96,128]{2,1,0:T(8,128)(2,1)S(1)}, bf16[8,96,128]{2,1,0:T(8,128)(2,1)S(1)}, u32[]{:S(2)}, u32[]{:S(2)}) %collective-permute-start.2) | collective-permute-done | bytes 196640 | tf_op jit(solution)/shard_map/ppermute | solution.py:233
  36.8 0.0 copy-start.2
  36.8 0.1 collective-permute-start.4
  36.9 0.0 collective-permute-done.3.came_ref
  37.0 7.7 %collective-permute-done.4 = bf16[8,96,128]{2,1,0:T(8,128)(2,1)S(1)} collective-permute-done((bf16[8,96,128]{2,1,0:T(8,128)(2,1)S(1)}, bf16[8,96,128]{2,1,0:T(8,128)(2,1)S(1)}, u32[]{:S(2)}, u32[]{:S(2)}) %collective-permute-start.4) | collective-permute-done | bytes 196640 | tf_op jit(solution)/shard_map/ppermute | solution.py:233
  44.7 0.0 copy-done.2
  44.7 0.8 %add_convert_fusion = bf16[8,96,128]{2,1,0:T(8,128)(2,1)} fusion(f32[8,96,128]{2,1,0:T(8,128)S(1)} %presum.1, bf16[8,96,128]{2,1,0:T(8,128)(2,1)S(1)} %collective-permute-done.4, f32[128]{0:T(128)S(1)} %copy-done.2), kind=kLoop, calls=%fused_computation | loop fusion | flops 491520 | bytes 786944 | tf_op jit(solution)/shard_map/convert_element_type | solution.py:263
  (3 shorter events, 0.1 us)
Async XLA Ops:
  0.0 10.7 %copy-start = (bf16[128,96,32]{0,2,1:T(8,128)(2,1)S(1)}, bf16[128,96,32]{0,2,1:T(8,128)(2,1)}, u32[]{:S(2)}) copy-start(bf16[128,96,32]{0,2,1:T(8,128)(2,1)} %param.5) | copy-start | bytes 2359300
  1.7 19.3 %all-to-all-start = ((bf16[32,2,32,128]{3,2,1,0:T(8,128)(2,1)}), bf16[32,2,32,128]{3,2,1,0:T(8,128)(2,1)S(1)}, u32[]{:S(2)}, u32[]{:S(2)}) async-start(bf16[32,2,32,128]{3,2,1,0:T(8,128)(2,1)} %spread.1), calls=%async_computation | async-start | bytes 1048576 | tf_op jit(solution)/shard_map/all_to_all | solution.py:243
  10.7 2.4 %collective-permute-start = (bf16[96,32,128]{2,1,0:T(8,128)(2,1)S(1)}, bf16[96,32,128]{2,1,0:T(8,128)(2,1)S(1)}, u32[]{:S(2)}, u32[]{:S(2)}) collective-permute-start(bf16[96,32,128]{2,1,0:T(8,128)(2,1)S(1)} %bitcast.11), channel_id=1, source_target_pairs={{0,32},{32,0},{1,33},{33,1},{2,34},{34,2},{3,35},{35,3},{4,36},{36... | collective-permute-start | bytes 2359304 | tf_op jit(solution)/shard_map/ppermute | solution.py:242
  21.0 1.0 %copy-start.1 = (bf16[1024,128]{1,0:T(8,128)(2,1)S(1)}, bf16[1024,128]{1,0:T(8,128)(2,1)}, u32[]{:S(2)}) copy-start(bf16[1024,128]{1,0:T(8,128)(2,1)} %matrix_ref.1) | copy-start | bytes 786436
  21.1 1.6 %collective-permute-start.1 = (bf16[4,8,32,128]{3,2,1,0:T(8,128)(2,1)S(1)}, bf16[4,8,32,128]{3,2,1,0:T(8,128)(2,1)S(1)}, u32[]{:S(2)}, u32[]{:S(2)}) collective-permute-start(bf16[4,8,32,128]{3,2,1,0:T(8,128)(2,1)S(1)} %select.1), channel_id=1, source_target_pairs={{0,32},{32,0},{1,33},{33,1},{2,34},{34,2},{3,35},{35,3},{4,36},{36... | collective-permute-start | bytes 786440 | tf_op jit(solution)/shard_map/ppermute | solution.py:250
  23.8 12.9 %collective-permute-start.2 = (bf16[8,96,128]{2,1,0:T(8,128)(2,1)S(1)}, bf16[8,96,128]{2,1,0:T(8,128)(2,1)S(1)}, u32[]{:S(2)}, u32[]{:S(2)}) collective-permute-start(bf16[8,96,128]{2,1,0:T(8,128)(2,1)S(1)} %pair_block.4), channel_id=1, source_target_pairs={{0,64},{16,208},{32,224},{48,112},{64,128},{80,16},{96,32},{112,17... | collective-permute-start | bytes 589832 | tf_op jit(solution)/shard_map/ppermute | solution.py:233
  28.3 8.6 %collective-permute-start.3 = (bf16[8,96,128]{2,1,0:T(8,128)(2,1)S(1)}, bf16[8,96,128]{2,1,0:T(8,128)(2,1)S(1)}, u32[]{:S(2)}, u32[]{:S(2)}) collective-permute-start(bf16[8,96,128]{2,1,0:T(8,128)(2,1)S(1)} %pair_block.7), channel_id=1, source_target_pairs={{0,96},{16,240},{32,192},{48,80},{64,160},{80,48},{96,0},{112,144}... | collective-permute-start | bytes 589832 | tf_op jit(solution)/shard_map/ppermute | solution.py:233
  36.8 7.9 %copy-start.2 = (f32[128]{0:T(128)S(1)}, f32[128]{0:T(128)}, u32[]{:S(2)}) copy-start(f32[128]{0:T(128)} %param.7) | copy-start | bytes 1540
  36.8 7.9 %collective-permute-start.4 = (bf16[8,96,128]{2,1,0:T(8,128)(2,1)S(1)}, bf16[8,96,128]{2,1,0:T(8,128)(2,1)S(1)}, u32[]{:S(2)}, u32[]{:S(2)}) collective-permute-start(bf16[8,96,128]{2,1,0:T(8,128)(2,1)S(1)} %merge.1), channel_id=1, source_target_pairs={{0,64},{16,208},{32,224},{48,112},{64,128},{80,16},{96,32},{112,17... | collective-permute-start | bytes 589832 | tf_op jit(solution)/shard_map/ppermute | solution.py:233
